TPU v7x, 128 devices: a whole 4x4x4 slice. The times are simulated.
128 devices in a mesh: row: 8 (over z, x_hi), col: 16 (over y, x_lo, core).
Axes of the slice: x: 4 (x_hi: 2, x_lo: 2; x = x_hi * 2 + x_lo), y: 4, z: 4, core: 2. Of those that a mesh axis runs over, the one named last changes fastest.
Arguments:
- atoms: bfloat16 [32768, 128], P(('row', 'col')), may hold values from -6 to 6
- tokens: bfloat16 [4096, 768], P('row', 'col'), may hold values from -6 to 6
- atom_bias: bfloat16 [1024, 4, 32, 128], P(('row', 'col')), may hold values from -7.5 to 250
- token_bias: bfloat16 [16, 4096, 4096], P(None, 'row', 'col'), may hold values from -8 to 250
- atom_index: int32 [32768], P(('row', 'col')), may hold values from 0 to 4095, as said below
- atom_counts: int32 [4096], P('row'), may hold values from 1 to 15, as said below
- window_starts: int32 [1024], P(('row', 'col')), may hold values from 0 to 32640, as said below
- gain_atom: float32 [128], replicated, may hold values from 0.5 to 1.5
- w_atom_q: bfloat16 [128, 128], replicated, may hold values from -0.5 to 0.5
- w_atom_kv: bfloat16 [128, 256], replicated, may hold values from -0.5 to 0.5
- w_atom_o: bfloat16 [128, 128], replicated, may hold values from -0.5 to 0.5
- w_agg: bfloat16 [128, 768], replicated, may hold values from -0.5 to 0.5
- gain_token: float32 [768], replicated, may hold values from 0.5 to 1.5
- w_query: bfloat16 [768, 768], replicated, may hold values from -0.21875 to 0.21875
- w_keyval: bfloat16 [768, 1536], replicated, may hold values from -0.21875 to 0.21875
- w_gate: bfloat16 [768, 768], replicated, may hold values from -0.21875 to 0.21875
- w_out: bfloat16 [768, 768], replicated, may hold values from -0.21875 to 0.21875
- w_t2a: bfloat16 [768, 128], replicated, may hold values from -0.21875 to 0.21875
- atoms_cot: bfloat16 [32768, 128], P(('row', 'col')), may hold values from -6 to 6
- tokens_cot: bfloat16 [4096, 768], P('row', 'col'), may hold values from -6 to 6
Outputs:
- atoms_out: bfloat16 [32768, 128], P(('row', 'col'))
- tokens_out: bfloat16 [4096, 768], P('row', 'col')
- grad_atoms: bfloat16 [32768, 128], P(('row', 'col'))
- grad_tokens: bfloat16 [4096, 768], P('row', 'col')
Inputs may be any that keep to these rules, and one draw needn't show every extreme that they name: atom_index never falls and names each token t exactly atom_counts[t] times. `atom_counts`: the counts of each aligned run of 512 tokens sum to 4096. window_starts[b] = min(max(32 * b - 48 + o_b, 0), 32640) with o_b an integer in -16 to 16; every window therefore reaches at most 64 atoms past the atoms of the device that holds block b.
All inputs are finite; a program needn't handle non-finite values.
Results may differ from a plain program's by a relative error of at most 0.013.
Values may be sent and summed in bfloat16 or wider, within the bound.
No kernel may reach another device: no remote copies, remote signals or barrier semaphores. Data moves between devices by JAX's collectives and lax.ppermute only.
A program may use at most 192 MiB of HBM per device.

v0:
```python
import math

import jax
import jax.numpy as jnp
from jax import lax
from jax.experimental import pallas as pl
from jax.experimental.pallas import tpu as pltpu
from jax.sharding import PartitionSpec as P

D = 768
H = 16
HD = 48
DA = 128
AH = 4
AHD = 32
QBLK = 32
KWIN = 128
RIM = 64
EPS = 1e-05
BF = jnp.bfloat16
F32 = jnp.float32
GROUP = 8
CORES = 2
CHUNK = 128
VMEM_LIMIT = 24 * 1024 * 1024
SMALL_LIMIT = 14 * 1024 * 1024


def dot(a, b):
    return jnp.dot(a, b, preferred_element_type=F32)


def dot_t(a, b):
    return lax.dot_general(a, b, (((1,), (1,)), ((), ())), preferred_element_type=F32)


def centred(values):
    center = values - jnp.mean(values, axis=-1, keepdims=True)
    inv = lax.rsqrt(jnp.mean(center * center, axis=-1, keepdims=True) + EPS)
    return center * inv, inv


def layer_norm(values, gain_vec):
    return centred(values)[0] * gain_vec


def norm_back(values, gain_vec, cotangent):
    unit, inv = centred(values)
    g = cotangent * gain_vec
    return inv * (
        g
        - jnp.mean(g, axis=-1, keepdims=True)
        - unit * jnp.mean(g * unit, axis=-1, keepdims=True)
    )


def sigmoid(x):
    return 1.0 / (1.0 + jnp.exp(-x))


def exchange(x, axis):
    return lax.all_to_all(x, axis, 0, 0)


def among_core(x):
    cols = lax.axis_size("col")
    groups = [list(range(core, cols, CORES)) for core in range(CORES)]
    return lax.all_to_all(x, "col", 0, 0, axis_index_groups=groups)


def halves_of(x):
    cols = lax.axis_size("col")
    mine = among_core(x)
    theirs = lax.ppermute(mine, "col", [(i, i ^ 1) for i in range(cols)])
    return mine, theirs


def neighbours(x, width):
    axes = ("row", "col")
    devices = lax.axis_size("row") * lax.axis_size("col")
    up = [(i, i + 1) for i in range(devices - 1)]
    down = [(j, i) for i, j in up]
    before = lax.ppermute(x[x.shape[0] - width :], axes, up)
    after = lax.ppermute(x[:width], axes, down)
    return before, after


def slab(k, count):
    return k % CORES * (count // CORES) + k // CORES


def rows_dot(a, b):
    return lax.dot_general(a, b, (((0,), (0,)), ((), ())), preferred_element_type=F32)


def head_window(head):
    start = head * HD
    low = start // 128 * 128
    high = -(-(start + HD) // 128) * 128
    return start, low, high


def widened(x_t, head):
    start, low, high = head_window(head)
    parts = []
    if start > low:
        parts.append(jnp.zeros((start - low, x_t.shape[1]), x_t.dtype))
    parts.append(x_t[start : start + HD])
    if high > start + HD:
        parts.append(jnp.zeros((high - start - HD, x_t.shape[1]), x_t.dtype))
    return jnp.concatenate(parts, axis=0)


def project_kernel(parts, normed, wt2a, wq, wg, wout, gate, gated, grad_new, both):
    cols = parts.shape[0]
    width = D // cols
    for k in range(cols):
        at = slice(k * width, (k + 1) * width)
        grad_new[:, at] = parts[k, :, DA + width : DA + 2 * width].astype(F32)
    cot = summed(parts[:, :, :DA]).astype(BF)
    grad_new[...] = grad_new[...] + dot_t(cot, wt2a[...])
    query = dot(normed[...], wq[...]).astype(BF)
    opened = sigmoid(dot(normed[...], wg[...]))
    grad = dot_t(grad_new[...].astype(BF), wout[...])
    gate[...] = opened
    gated[...] = grad
    grad = (grad * opened).astype(BF)
    for k in range(both.shape[0]):
        both[k, :, :D] = query
        both[k, :, D:] = grad


def token_project(parts, normed, w_t2a, w_query, w_gate, w_out, copies):
    cols, own, _ = parts.shape
    last = D // (2 * DA)
    full = lambda *shape: pl.BlockSpec(shape, lambda i: (0,) * len(shape))
    return pl.pallas_call(
        project_kernel,
        grid=(1,),
        in_specs=[
            pl.BlockSpec((cols, own, 2 * DA), lambda i: (0, 0, last)),
            full(own, D),
            full(D, DA),
            full(D, D),
            full(D, D),
            full(D, D),
        ],
        out_specs=[full(own, D), full(own, D), full(own, D), full(copies, own, 2 * D)],
        out_shape=[
            pltpu.HBM((own, D), F32),
            pltpu.HBM((own, D), F32),
            pltpu.HBM((own, D), F32),
            pltpu.HBM((copies, own, 3 * D), BF),
        ],
        compiler_params=pltpu.CompilerParams(vmem_limit_bytes=SMALL_LIMIT),
        name="token_project",
    )(parts, far(normed), far(w_t2a), w_query, w_gate, w_out)


def pack_kernel(packed, keys, out):
    out[...] = keys[...]


def token_pack(packed, keys):
    return pl.pallas_call(
        pack_kernel,
        grid=(1,),
        in_specs=[
            pl.BlockSpec(memory_space=pl.ANY),
            pl.BlockSpec(keys.shape, lambda i: (0, 0, 0)),
        ],
        out_specs=pl.BlockSpec(keys.shape, lambda i: (0, 0, 2)),
        out_shape=pltpu.HBM(packed.shape, BF),
        input_output_aliases={0: 0},
        compiler_params=pltpu.CompilerParams(vmem_limit_bytes=SMALL_LIMIT),
        name="token_pack",
    )(packed, keys)


def key_kernel(key_normed, wk, wv, k_t, v_t):
    k_t[...] = dot(key_normed[...], wk[...]).astype(BF).T
    v_t[...] = dot(key_normed[...], wv[...]).astype(BF).T


def token_keys(mine, w_keyval):
    tok_col = mine.shape[0]
    span = GROUP * HD
    groups = H // GROUP
    return pl.pallas_call(
        key_kernel,
        grid=(groups,),
        in_specs=[
            pl.BlockSpec((tok_col, D), lambda i: (0, 2)),
            pl.BlockSpec((D, span), lambda i: (0, i)),
            pl.BlockSpec((D, span), lambda i: (0, groups + i)),
        ],
        out_specs=[pl.BlockSpec((span, tok_col), lambda i: (i, 0)) for _ in range(2)],
        out_shape=[pltpu.HBM((D, tok_col), BF) for _ in range(2)],
        compiler_params=pltpu.CompilerParams(vmem_limit_bytes=SMALL_LIMIT),
        name="token_keys",
    )(mine, far(w_keyval), far(w_keyval))


def forward_kernel(
    core, k_t, v_t, q_mine, q_theirs, g_mine, g_theirs, bias,
    q, q_t, g, g_t, mixed, stats, exps, out_t,
):
    half = q_mine.shape[0]
    mine = pl.ds(pl.multiple_of(core[0] * half, half), half)
    theirs = pl.ds(pl.multiple_of((1 - core[0]) * half, half), half)
    q[mine, :] = q_mine[...]
    q[theirs, :] = q_theirs[...]
    g[mine, :] = g_mine[...]
    g[theirs, :] = g_theirs[...]
    q_t[...] = q[...].T
    g_t[...] = g[...].T
    copies = stats.shape[0]
    rows = q.shape[0]
    scale = 1.0 / math.sqrt(HD)
    keys = k_t[...]
    values = v_t[...]
    lane = lax.broadcasted_iota(jnp.int32, (CHUNK, 128), 1)
    tops = [jnp.zeros((CHUNK, 128), F32) for _ in range(rows // CHUNK)]
    totals = []
    deltas = []
    for head in range(GROUP):
        start, low, high = head_window(head)
        wide = widened(keys, head)
        for part in range(rows // CHUNK):
            at = pl.ds(part * CHUNK, CHUNK)
            score = dot(q[at, low:high], wide) * scale + bias[head, at, :].astype(F32)
            top = jnp.max(score, axis=1, keepdims=True)
            exps[at, :] = jnp.exp(score - top).astype(BF)
            tops[part] = jnp.where(lane == head, top, tops[part])
        ones = jnp.ones((16, values.shape[1]), BF)
        weighted = dot_t(jnp.concatenate([values[start : start + HD], ones], axis=0), exps[...])
        total = weighted[HD : HD + 1]
        one = weighted[:HD] / total
        out_t[start : start + HD, :] = one
        totals.append(total)
        deltas.append(
            jnp.sum(g_t[start : start + HD, :].astype(F32) * one, axis=0, keepdims=True)
        )
    tops_t = jnp.concatenate(tops, axis=0).T[:GROUP]
    lse = tops_t + jnp.log(jnp.concatenate(totals, axis=0))
    delta = jnp.concatenate(deltas, axis=0)
    high = lse.astype(BF).astype(F32)
    middle = (lse - high).astype(BF).astype(F32)
    triple = jnp.concatenate([high, middle, delta], axis=0).astype(BF)
    for copy in range(copies):
        stats[copy, 0] = triple
    straight = out_t[...].astype(BF).T
    cols, own, _ = mixed.shape
    for k in range(cols):
        at = slice(slab(k, cols) * own, (slab(k, cols) + 1) * own)
        mixed[k] = straight[at]


def token_forward(core, k_t, v_t, mine, theirs, bias, cols):
    copies = cols // CORES
    half = mine.shape[0]
    tok_col = half
    rows = CORES * half
    span = GROUP * HD
    groups = H // GROUP
    return pl.pallas_call(
        forward_kernel,
        grid=(groups,),
        in_specs=[
            pl.BlockSpec(memory_space=pltpu.SMEM),
            pl.BlockSpec((span, tok_col), lambda i: (i, 0)),
            pl.BlockSpec((span, tok_col), lambda i: (i, 0)),
            pl.BlockSpec((half, span), lambda i: (0, i)),
            pl.BlockSpec((half, span), lambda i: (0, i)),
            pl.BlockSpec((half, span), lambda i: (0, groups + i)),
            pl.BlockSpec((half, span), lambda i: (0, groups + i)),
            pl.BlockSpec((GROUP, rows, tok_col), lambda i: (i, 0, 0)),
        ],
        out_specs=[
            pl.BlockSpec((rows, span), lambda i: (0, i)),
            pl.BlockSpec((span, rows), lambda i: (i, 0)),
            pl.BlockSpec((rows, span), lambda i: (0, i)),
            pl.BlockSpec((span, rows), lambda i: (i, 0)),
            pl.BlockSpec((cols, rows // cols, span), lambda i: (0, 0, i)),
            pl.BlockSpec((copies, 1, 3 * GROUP, rows), lambda i: (0, i, 0, 0)),
        ],
        out_shape=[
            pltpu.HBM((rows, D), BF),
            pltpu.HBM((D, rows), BF),
            pltpu.HBM((rows, D), BF),
            pltpu.HBM((D, rows), BF),
            pltpu.HBM((cols, rows // cols, D), BF),
            pltpu.HBM((copies, groups, 3 * GROUP, rows), BF),
        ],
        scratch_shapes=[pltpu.VMEM((rows, tok_col), BF), pltpu.VMEM((span, rows), F32)],
        compiler_params=pltpu.CompilerParams(vmem_limit_bytes=VMEM_LIMIT),
        name="token_forward",
    )(core, far(k_t), far(v_t), mine, theirs, mine, theirs, far(bias))


def backward_kernel(
    core, mine, theirs, q, q_t, g, g_t, k_t, v_t, bias, wk, wv, q_mine, q_theirs, kv_feat,
    probs, slopes, q_acc, k_acc, v_acc, straight, feat,
):
    rows = q.shape[0]
    tok_col = k_t.shape[1]
    scale = 1.0 / math.sqrt(HD)
    logs = []
    deltas = []
    for part in (mine, theirs):
        for k in range(part.shape[0]):
            triple = part[k, 0].astype(F32)
            logs.append(triple[:GROUP] + triple[GROUP : 2 * GROUP])
            deltas.append(triple[2 * GROUP :])
    top = logs[0]
    for one in logs[1:]:
        top = jnp.maximum(top, one)
    share_sum = jnp.zeros_like(top)
    delta = jnp.zeros_like(top)
    for one, other in zip(logs, deltas):
        share = jnp.exp(one - top)
        share_sum = share_sum + share
        delta = delta + share * other
    lse = top + jnp.log(share_sum)
    delta = delta / share_sum
    filler = jnp.zeros((128 - 2 * GROUP, rows), F32)
    columns = jnp.concatenate([lse, delta, filler], axis=0).T
    for head in range(GROUP):
        start, low, high = head_window(head)
        wide_k = widened(k_t[...], head)
        wide_v = widened(v_t[...], head)
        for part in range(rows // CHUNK):
            at = pl.ds(part * CHUNK, CHUNK)
            some = columns[part * CHUNK : (part + 1) * CHUNK]
            score = dot(q[at, low:high], wide_k) * scale + bias[head, at, :].astype(F32)
            prob = jnp.exp(score - some[:, head : head + 1])
            grad = dot(g[at, low:high], wide_v) - some[:, GROUP + head : GROUP + head + 1]
            probs[at, :] = prob.astype(BF)
            slopes[at, :] = (prob * grad).astype(BF)
        here = pl.ds(start, HD)
        k_acc[here, :] = dot(q_t[here, :], slopes[...]) * scale
        v_acc[here, :] = dot(g_t[here, :], probs[...])
        q_acc[here, :] = dot_t(k_t[here, :], slopes[...]) * scale
    new = dot(wk[...], k_acc[...].astype(BF)) + dot(wv[...], v_acc[...].astype(BF))

    @pl.when(pl.program_id(0) == 0)
    def _():
        feat[...] = new

    @pl.when(pl.program_id(0) > 0)
    def _():
        kv_feat[...] = (feat[...] + new).astype(BF).T

    straight[...] = q_acc[...].astype(BF).T
    half = q_mine.shape[0]
    q_mine[...] = straight[pl.ds(pl.multiple_of(core[0] * half, half), half), :]
    q_theirs[...] = straight[pl.ds(pl.multiple_of((1 - core[0]) * half, half), half), :]


def token_backward(core, mine, theirs, q, q_t, g, g_t, k_t, v_t, bias, w_keyval):
    rows = q.shape[0]
    tok_col = k_t.shape[1]
    parts = mine.shape[0]
    half = rows // CORES
    groups = H // GROUP
    span = GROUP * HD
    straight = lambda: pl.BlockSpec((rows, span), lambda i: (0, i))
    turned = lambda: pl.BlockSpec((span, rows), lambda i: (i, 0))
    keyed = lambda: pl.BlockSpec((span, tok_col), lambda i: (i, 0))
    return pl.pallas_call(
        backward_kernel,
        grid=(groups,),
        in_specs=[
            pl.BlockSpec(memory_space=pltpu.SMEM),
            pl.BlockSpec((parts, 1, 3 * GROUP, rows), lambda i: (0, i, 0, 0)),
            pl.BlockSpec((parts, 1, 3 * GROUP, rows), lambda i: (0, i, 0, 0)),
            straight(),
            turned(),
            straight(),
            turned(),
            keyed(),
            keyed(),
            pl.BlockSpec((GROUP, rows, tok_col), lambda i: (i, 0, 0)),
            pl.BlockSpec((D, span), lambda i: (0, i)),
            pl.BlockSpec((D, span), lambda i: (0, groups + i)),
        ],
        out_specs=[
            pl.BlockSpec((half, span), lambda i: (0, i)),
            pl.BlockSpec((half, span), lambda i: (0, i)),
            pl.BlockSpec((tok_col, D), lambda i: (0, 0)),
        ],
        out_shape=[
            pltpu.HBM((half, D), BF),
            pltpu.HBM((half, D), BF),
            pltpu.HBM((tok_col, D), BF),
        ],
        scratch_shapes=[
            pltpu.VMEM((rows, tok_col), BF),
            pltpu.VMEM((rows, tok_col), BF),
            pltpu.VMEM((span, rows), F32),
            pltpu.VMEM((span, tok_col), F32),
            pltpu.VMEM((span, tok_col), F32),
            pltpu.VMEM((rows, span), BF),
            pltpu.VMEM((D, tok_col), F32),
        ],
        compiler_params=pltpu.CompilerParams(vmem_limit_bytes=VMEM_LIMIT),
        name="token_backward",
    )(
        core,
        mine,
        theirs,
        far(q),
        far(q_t),
        far(g),
        far(g_t),
        far(k_t),
        far(v_t),
        far(bias),
        far(w_keyval),
        far(w_keyval),
    )


def far(x):
    return pltpu.with_memory_space_constraint(x, pltpu.HBM)


def shaped(shape, dtype):
    return jax.ShapeDtypeStruct(shape, dtype)


def whole(kernel, outs, args, name, scalars=0, scratch=()):
    specs = [pl.BlockSpec(memory_space=pltpu.SMEM)] * scalars
    specs += [pl.BlockSpec(memory_space=pltpu.VMEM)] * (len(args) - scalars)
    return pl.pallas_call(
        kernel,
        in_specs=specs,
        out_specs=[pl.BlockSpec(memory_space=pltpu.VMEM)] * len(outs),
        out_shape=list(outs),
        scratch_shapes=list(scratch),
        compiler_params=pltpu.CompilerParams(vmem_limit_bytes=SMALL_LIMIT),
        name=name,
    )(*args)


def head_lanes(head):
    lane = lax.broadcasted_iota(jnp.int32, (1, DA), 1)
    return (lane >= head * AHD) & (lane < (head + 1) * AHD)


def stacked(x):
    return jnp.concatenate(
        [jnp.where(head_lanes(head), x, jnp.zeros_like(x)) for head in range(AH)], axis=0
    )


def unstacked(x):
    total = jnp.zeros((QBLK, DA), F32)
    for head in range(AH):
        total = jnp.where(head_lanes(head), x[head * QBLK : (head + 1) * QBLK], total)
    return total


def picked(start, padded_rows):
    row = lax.broadcasted_iota(jnp.int32, (KWIN, padded_rows), 0)
    lane = lax.broadcasted_iota(jnp.int32, (KWIN, padded_rows), 1)
    return jnp.where(row + start == lane, 1.0, 0.0).astype(BF)


def atoms_forward_kernel(
    starts, before, atoms, after, bias, token, gain, wq, wkv, wo, wagg, cot, tokens, tokens_cot,
    part, mid, slope, query, window, prob, mixed,
):
    atom_dev = atoms.shape[0]
    blocks = window.shape[0]
    cols, own, _ = part.shape
    tok_row = cols * own
    scale = 1.0 / math.sqrt(AHD)
    padded = jnp.concatenate([before[...], atoms[...], after[...]], axis=0).astype(F32)
    padded_rows = padded.shape[0]
    normed = layer_norm(padded, gain[...]).astype(BF)
    query[...] = dot(normed[RIM : RIM + atom_dev], wq[...]).astype(BF)
    keyval = dot(normed, wkv[...]).astype(BF)
    for block in range(blocks):
        at = pl.ds(block * QBLK, QBLK)
        rows = dot(picked(starts[block], padded_rows), keyval).astype(BF)
        window[block] = rows
        score = dot_t(stacked(query[at, :]), rows[:, :DA]) * scale + bias[block].astype(F32)
        exps = jnp.exp(score - jnp.max(score, axis=-1, keepdims=True))
        one = exps / jnp.sum(exps, axis=-1, keepdims=True)
        prob[block] = one
        mixed[at, :] = unstacked(dot(one.astype(BF), rows[:, DA:])).astype(BF)
    mid[...] = (atoms[...].astype(F32) + dot(mixed[...], wo[...])).astype(BF)
    slot = lax.broadcasted_iota(jnp.int32, (tok_row, atom_dev), 0)
    member = jnp.where(slot == token[...], 1.0, 0.0).astype(BF)
    width = tokens.shape[0]
    cot_part = dot(member, cot[...]).astype(BF)
    blank = jnp.zeros((part.shape[2] - D - DA - 2 * width, tok_row), BF)
    rest = jnp.concatenate([tokens[...], tokens_cot[...], blank], axis=0).T
    for k in range(cols):
        at = slice(slab(k, cols) * own, (slab(k, cols) + 1) * own)
        part[k, :, D : D + DA] = cot_part[at]
        part[k, :, D + DA :] = rest[at]
    for low in range(0, D, 256):
        at = pl.ds(low, 256)
        pre = dot(mid[...], wagg[:, at])
        gate = sigmoid(pre)
        slope[:, at] = gate * (1.0 + pre * (1.0 - gate))
        sums = dot(member, (pre * gate).astype(BF)).astype(BF)
        for k in range(cols):
            part[k, :, at] = sums[slab(k, cols) * own : (slab(k, cols) + 1) * own]


def summed(parts):
    total = parts[0].astype(F32)
    for k in range(1, parts.shape[0]):
        total = total + parts[k].astype(F32)
    return total


def norm_kernel(parts, inverse, gain, mid, normed, spread):
    cols = parts.shape[0]
    width = D // cols
    low = D + DA
    for k in range(cols):
        mid[:, k * width : (k + 1) * width] = parts[k, :, low : low + width].astype(F32)
    value = mid[...] + summed(parts[:, :, :D]) * inverse[...]
    mid[...] = value
    out = layer_norm(value, gain[...]).astype(BF)
    normed[...] = out
    for k in range(spread.shape[0]):
        spread[k] = out


def keyval_kernel(parts, out):
    out[...] = summed(parts[...]).astype(BF)


def own_kernel(
    place, parts, mine, theirs, gate_ref, gated_ref, token_mid, wout, wgate, wt2a, tokens, lifted, feature, attended
):
    cols, own, _ = parts.shape
    span = GROUP * HD
    lane = lax.broadcasted_iota(jnp.int32, (GROUP, span), 1)
    row = lax.broadcasted_iota(jnp.int32, (GROUP, span), 0)
    widen = jnp.where((lane >= row * HD) & (lane < (row + 1) * HD), 1.0, 0.0).astype(BF)
    half = cols // CORES
    rows = mine.shape[3]
    slot = lax.broadcasted_iota(jnp.int32, (rows, own), 0)
    token = lax.broadcasted_iota(jnp.int32, (rows, own), 1)
    select = jnp.where(slot == token + place[0], 1.0, 0.0).astype(BF)
    tables = []
    for part in (mine, theirs):
        flat = part[...].reshape(half * (H // GROUP) * 3 * GROUP, rows)
        tables.append(dot(flat, select).T)
    for group in range(H // GROUP):
        logs = []
        for k in range(cols):
            low = (k // CORES * (H // GROUP) + group) * 3 * GROUP
            mine_first = jnp.where(place[1] == k % CORES, 1.0, 0.0)
            triple = (
                tables[0][:, low : low + 2 * GROUP] * mine_first
                + tables[1][:, low : low + 2 * GROUP] * (1.0 - mine_first)
            )
            logs.append(triple[:, :GROUP] + triple[:, GROUP:])
        top = logs[0]
        for k in range(1, cols):
            top = jnp.maximum(top, logs[k])
        shares = [jnp.exp(one - top) for one in logs]
        total = shares[0]
        for k in range(1, cols):
            total = total + shares[k]
        share = jnp.concatenate([one / total for one in shares], axis=0)
        high = share.astype(BF)
        rest = (share - high.astype(F32)).astype(BF)
        weight = dot(high, widen) + dot(rest, widen)
        value = jnp.zeros((own, span), F32)
        for k in range(cols):
            at = slice(group * span, (group + 1) * span)
            value = value + weight[k * own : (k + 1) * own] * parts[k, :, at].astype(F32)
        attended[:, group * span : (group + 1) * span] = value
    gate = gate_ref[...]
    value = attended[...]
    new = (token_mid[...] + dot((gate * value).astype(BF), wout[...])).astype(BF)
    tokens[...] = new
    lifted[...] = dot(new, wt2a[...]).astype(BF)
    grad_gate = (gated_ref[...] * value * gate * (1.0 - gate)).astype(BF)
    feature[...] = dot_t(grad_gate, wgate[...])


def token_kernel(parts, key_feature, feature, grad_new, token_mid, gain, wquery, tokens, lifted, out):
    cols = CORES * parts.shape[0]
    width = D // cols
    total = summed(parts[...]).astype(BF)
    normed_grad = dot_t(total, wquery[...]) + feature[...] + key_feature[...].astype(F32)
    grad = grad_new[...] + norm_back(token_mid[...], gain[...], normed_grad)
    grad = grad.astype(BF)
    new = tokens[...]
    low = D + DA
    pair = CORES * width
    for k in range(cols // CORES):
        out[k, :, :D] = grad
        out[k, :, D:low] = lifted[...]
        out[k, :, low:] = new[:, k * pair : (k + 1) * pair]


def atoms_backward_kernel(
    starts, place, mine, theirs, token, inverse, slope, cot, mid, query, window, prob, mixed,
    wagg, wo, wq, new, tokens_out, grad_tokens, inner, first, last, atoms_grad, feature, padded,
):
    atom_dev = cot.shape[0]
    blocks = window.shape[0]
    half = mine.shape[0]
    tok_row = CORES * half
    width = tokens_out.shape[1]
    core = place[0]
    padded_rows = padded.shape[0]
    scale = 1.0 / math.sqrt(AHD)
    slot = lax.broadcasted_iota(jnp.int32, (atom_dev, tok_row), 1)
    atom_inverse = jnp.sum(
        jnp.where(slot == token[...], inverse[...], 0.0), axis=1, keepdims=True
    )
    parts = ((mine, core * half), (theirs, (1 - core) * half))
    slot = lax.broadcasted_iota(jnp.int32, (atom_dev, half), 1)
    members = [
        jnp.where(slot + base == token[...], 1.0, 0.0).astype(BF) for _, base in parts
    ]

    def gathered(at):
        return dot(members[0], mine[:, at]) + dot(members[1], theirs[:, at])

    row = lax.broadcasted_iota(jnp.int32, (D, width), 0)
    lane = lax.broadcasted_iota(jnp.int32, (D, width), 1)
    column = jnp.where(row == lane + place[1] * width, 1.0, 0.0).astype(BF)
    for part, base in parts:
        here = pl.ds(pl.multiple_of(base, half), half)
        low = D + DA
        pair = part[:, low:].astype(F32)
        tokens_out[here, :] = jnp.where(core == 0, pair[:, :width], pair[:, width:]).astype(BF)
        grad_tokens[here, :] = dot(part[:, :D], column).astype(BF)
    grads = cot[...].astype(F32)
    for low in range(0, D, 256):
        at = pl.ds(low, 256)
        hidden = (gathered(at) * atom_inverse * slope[:, at]).astype(BF)
        grads = grads + dot_t(hidden, wagg[:, at])
    atoms_grad[...] = grads
    mixed_grad = dot_t(grads.astype(BF), wo[...]).astype(BF)
    padded[...] = jnp.zeros(padded.shape, F32)
    for block in range(blocks):
        at = slice(block * QBLK, (block + 1) * QBLK)
        rows = window[block]
        one = prob[block]
        grad_heads = stacked(mixed_grad[at])
        query_heads = stacked(query[at, :])
        grad_wide = grad_heads.astype(F32)
        tall = jnp.concatenate([mixed[at, :]] * AH, axis=0).astype(F32)
        delta = jnp.sum(grad_wide * tall, axis=-1, keepdims=True)
        sgrad = (one * (dot_t(grad_heads, rows[:, DA:]) - delta)).astype(BF)
        qgrad = (unstacked(dot(sgrad, rows[:, :DA])) * scale).astype(BF)
        feature[at, :] = dot_t(qgrad, wq[...])
        key_grad = rows_dot(sgrad, query_heads) * scale
        value_grad = rows_dot(one.astype(BF), grad_heads)
        both = jnp.concatenate([key_grad, value_grad], axis=1).astype(BF)
        padded[...] += rows_dot(picked(starts[block], padded_rows), both)
    first[...] = padded[:RIM, :].astype(BF)
    last[...] = padded[RIM + atom_dev :, :].astype(BF)
    inner[...] = padded[RIM : RIM + atom_dev, :]
    lift = gathered(slice(D, D + DA))
    new[...] = (mid[...].astype(F32) + lift).astype(BF)


def atoms_last_kernel(inner, before, after, feature, atoms_grad, atoms, gain, wkv, out):
    atom_dev = atoms.shape[0]
    keyval = jnp.concatenate(
        [
            inner[:RIM, :] + before[...].astype(F32),
            inner[RIM : atom_dev - RIM, :],
            inner[atom_dev - RIM :, :] + after[...].astype(F32),
        ],
        axis=0,
    ).astype(BF)
    feat = feature[...] + dot_t(keyval, wkv[...])
    back = norm_back(atoms[...].astype(F32), gain[...], feat)
    out[...] = (atoms_grad[...] + back).astype(BF)


def local(
    atoms,
    tokens,
    atom_bias,
    token_bias,
    atom_index,
    atom_counts,
    window_starts,
    gain_atom,
    w_atom_q,
    w_atom_kv,
    w_atom_o,
    w_agg,
    gain_token,
    w_query,
    w_keyval,
    w_gate,
    w_out,
    w_t2a,
    atoms_cot,
    tokens_cot,
):
    rows = lax.axis_size("row")
    cols = lax.axis_size("col")
    row_index = lax.axis_index("row")
    col_index = lax.axis_index("col")
    atom_dev = atoms.shape[0]
    blocks = window_starts.shape[0]
    tok_row = tokens.shape[0]
    tok_col = token_bias.shape[2]
    own = tok_row // cols
    width = tokens.shape[1]
    first_atom = (row_index * cols + col_index) * atom_dev

    before, after = neighbours(atoms, RIM)

    local_token = atom_index - row_index * tok_row
    inverse_count = 1.0 / atom_counts.astype(F32)
    core = col_index % CORES
    half = tok_row // CORES
    first_own = core * half + col_index // CORES * own
    inv_own = lax.dynamic_slice_in_dim(inverse_count, first_own, own, 0)

    starts = window_starts - first_atom + RIM
    gain_a = gain_atom[None, :]
    gain_t = gain_token[None, :]
    part, atoms_mid, slope, atom_query, window, atom_prob, atom_mixed = whole(
        atoms_forward_kernel,
        [
            pltpu.HBM((cols, own, D + 2 * DA), BF),
            pltpu.HBM((atom_dev, DA), BF),
            pltpu.HBM((atom_dev, D), F32),
            pltpu.HBM((atom_dev, DA), BF),
            pltpu.HBM((blocks, KWIN, 2 * DA), BF),
            pltpu.HBM((blocks, AH * QBLK, KWIN), F32),
            pltpu.HBM((atom_dev, DA), BF),
        ],
        (
            starts,
            before,
            far(atoms),
            after,
            far(atom_bias.reshape(blocks, AH * QBLK, KWIN)),
            local_token[None, :],
            gain_a,
            far(w_atom_q),
            far(w_atom_kv),
            far(w_atom_o),
            far(w_agg),
            far(atoms_cot),
            far(tokens.T),
            far(tokens_cot.T),
        ),
        "atoms_forward",
        scalars=1,
    )

    sums = exchange(part, "col")
    tokens_mid, normed_own, spread = whole(
        norm_kernel,
        [
            pltpu.HBM((own, D), F32),
            pltpu.HBM((own, D), BF),
            pltpu.HBM((rows, own, D), BF),
        ],
        (sums, inv_own[:, None], gain_t),
        "token_norm",
    )
    keys_own = exchange(spread, "row")
    gate_own, gated_own, grad_new, packed = token_project(
        sums, normed_own, w_t2a, w_query, w_gate, w_out, rows
    )
    packed = token_pack(packed, keys_own)
    mine, theirs = halves_of(packed)
    to_row = [
        (i * cols + r * CORES + p, r * cols + i * CORES + p)
        for r in range(rows)
        for i in range(rows)
        for p in range(CORES)
    ]
    k_t, v_t = token_keys(mine.reshape(half, 3 * D), w_keyval)
    q, q_t, g, g_t, mixed, stats = token_forward(
        core[None],
        k_t,
        v_t,
        mine.reshape(half, 3 * D),
        theirs.reshape(half, 3 * D),
        token_bias,
        cols,
    )
    stats = halves_of(stats)
    mixed_parts = exchange(mixed, "col")
    q_mine, q_theirs, kv_feat = token_backward(
        core[None], *stats, q, q_t, g, g_t, k_t, v_t, token_bias, w_keyval
    )
    swap = [(i, i ^ 1) for i in range(cols)]
    q_other = lax.ppermute(q_theirs, "col", swap)
    kv_parts = exchange(kv_feat.reshape(rows, own, D), "row")
    q_pair = (q_mine.astype(F32) + q_other.astype(F32)).astype(BF)
    q_parts = among_core(q_pair.reshape(cols // CORES, own, D))
    tokens_new, lifted, gate_feat = whole(
        own_kernel,
        [shaped((own, D), BF), shaped((own, DA), BF), shaped((own, D), F32)],
        (
            jnp.stack([first_own, core]),
            mixed_parts,
            *stats,
            far(gate_own),
            far(gated_own),
            far(tokens_mid),
            far(w_out),
            far(w_gate),
            far(w_t2a),
        ),
        "token_own",
        scalars=1,
        scratch=[pltpu.VMEM((own, D), F32)],
    )
    (kv_own,) = whole(
        keyval_kernel,
        [shaped((own, D), BF)],
        (kv_parts,),
        "token_keyval",
    )
    kv_back = lax.ppermute(kv_own, ("row", "col"), to_row)
    (mid_spread,) = whole(
        token_kernel,
        [pltpu.HBM((cols // CORES, own, D + DA + CORES * width), BF)],
        (
            q_parts,
            kv_back,
            gate_feat,
            far(grad_new),
            far(tokens_mid),
            gain_t,
            far(w_query),
            tokens_new,
            lifted,
        ),
        "token_grads",
    )
    mine, theirs = halves_of(mid_spread)

    atoms_new, tokens_out, grad_tokens, inner, first, last, atoms_grad, query_feat = whole(
        atoms_backward_kernel,
        [
            shaped((atom_dev, DA), BF),
            shaped((tok_row, width), BF),
            shaped((tok_row, width), BF),
            pltpu.HBM((atom_dev, 2 * DA), F32),
            shaped((RIM, 2 * DA), BF),
            shaped((RIM, 2 * DA), BF),
            pltpu.HBM((atom_dev, DA), F32),
            pltpu.HBM((atom_dev, DA), F32),
        ],
        (
            starts,
            jnp.stack([core, col_index]),
            mine.reshape(half, -1),
            theirs.reshape(half, -1),
            local_token[:, None],
            inverse_count[None, :],
            slope,
            far(atoms_cot),
            far(atoms_mid),
            far(atom_query),
            window,
            atom_prob,
            far(atom_mixed),
            far(w_agg),
            far(w_atom_o),
            far(w_atom_q),
        ),
        "atoms_backward",
        scalars=2,
        scratch=[pltpu.VMEM((atom_dev + 2 * RIM, 2 * DA), F32)],
    )
    axes = ("row", "col")
    up = [(i, i + 1) for i in range(rows * cols - 1)]
    down = [(j, i) for i, j in up]
    from_before = lax.ppermute(last, axes, up)
    from_after = lax.ppermute(first, axes, down)
    (grad_atoms,) = whole(
        atoms_last_kernel,
        [shaped((atom_dev, DA), BF)],
        (
            far(inner),
            from_before,
            from_after,
            far(query_feat),
            far(atoms_grad),
            far(atoms),
            gain_a,
            far(w_atom_kv),
        ),
        "atoms_last",
    )
    return (atoms_new, tokens_out, grad_atoms, grad_tokens)


def solution(mesh):
    placed = (
        P(("row", "col"), None),
        P("row", "col"),
        P(("row", "col"), None, None, None),
        P(None, "row", "col"),
        P(("row", "col")),
        P("row"),
        P(("row", "col")),
        P(),
        P(),
        P(),
        P(),
        P(),
        P(),
        P(),
        P(),
        P(),
        P(),
        P(),
        P(("row", "col"), None),
        P("row", "col"),
    )
    return jax.shard_map(
        local,
        mesh=mesh,
        in_specs=placed,
        out_specs=(
            P(("row", "col"), None),
            P("row", "col"),
            P(("row", "col"), None),
            P("row", "col"),
        ),
        check_vma=False,
    )
```

profile of v0, /device:TPU:31, one launch (start us, length us, event | category | flops | bytes accessed | tf_op | source)
XLA Modules:
  0.0 194.2 jit_solution(6885368922515091959)
XLA Ops:
  0.6 0.7 fusion
  1.4 3.7 %collective-permute-start = (bf16[64,128]{1,0:T(8,128)(2,1)S(1)}, bf16[64,128]{1,0:T(8,128)(2,1)S(1)}, u32[]{:S(2)}, u32[]{:S(2)}) collective-permute-start(bf16[64,128]{1,0:T(8,128)(2,1)S(1)} %get-tuple-element.85), channel_id=1, source_target_pairs={{0,1},{1,2},{2,3},{3,4},{4,5},{5,6},{6,7},{7,8},{8,9},{9,10},{10,1... | collective-permute-start | bytes 49160 | tf_op jit(solution)/shard_map/ppermute | solution.py:83
  5.0 1.9 collective-permute-start.1
  7.0 0.7 broadcast_subtract_fusion
  7.7 0.7 subtract_add_fusion.starts
  8.3 0.0 collective-permute-done.before
  8.3 6.0 %collective-permute-done.1.after = bf16[64,128]{1,0:T(8,128)(2,1)S(1)} collective-permute-done((bf16[64,128]{1,0:T(8,128)(2,1)S(1)}, bf16[64,128]{1,0:T(8,128)(2,1)S(1)}, u32[]{:S(2)}, u32[]{:S(2)}) %collective-permute-start.1) | collective-permute-done | bytes 16416 | tf_op jit(solution)/shard_map/ppermute | solution.py:84
  14.3 0.7 copy-done.6
  15.0 7.5 %atoms_forward.1 = (bf16[16,32,1024]{2,1,0:T(8,128)(2,1)}, bf16[256,128]{1,0:T(8,128)(2,1)}, f32[256,768]{1,0:T(8,128)}, bf16[256,128]{1,0:T(8,128)(2,1)}, bf16[...) custom-call(s32[8]{0:T(128)S(1)} %subtract_add_fusion.starts, ...), custom_call_target="tpu_custom_call" | custom-call | tf_op jit(solution)/shard_map/atoms_forward/pallas_call | solution.py:435
  22.4 0.0 copy-start.8
  22.5 0.0 copy-start.1
  22.5 5.3 %all-to-all-start = ((bf16[16,32,1024]{2,1,0:T(8,128)(2,1)}), bf16[16,32,1024]{2,1,0:T(8,128)(2,1)S(1)}, u32[]{:S(2)}, u32[]{:S(2)}) async-start(bf16[16,32,1024]{2,1,0:T(8,128)(2,1)} %get-tuple-element.40), calls=%async_computation | async-start | bytes 2097152 | tf_op jit(solution)/shard_map/all_to_all | solution.py:62
  27.8 0.0 copy-done.9
  27.9 0.1 dynamic-slice_bitcast_fusion
  27.9 0.1 copy.28.inverse
  28.0 0.0 copy-done.8
  28.0 12.4 %all-to-all-done.parts = bf16[16,32,1024]{2,1,0:T(8,128)(2,1)S(1)} async-done(((bf16[16,32,1024]{2,1,0:T(8,128)(2,1)}), bf16[16,32,1024]{2,1,0:T(8,128)(2,1)S(1)}, u32[]{:S(2)}, u32[]{:S(2)}) %all-to-all-start) | async-done | bytes 1048608 | tf_op jit(solution)/shard_map/all_to_all | solution.py:62
  40.5 1.1 token_norm.1
  41.6 7.3 %all-to-all-start.1 = ((bf16[8,32,768]{2,1,0:T(8,128)(2,1)}), bf16[8,32,768]{2,1,0:T(8,128)(2,1)}, u32[]{:S(2)}, u32[]{:S(2)}) async-start(bf16[8,32,768]{2,1,0:T(8,128)(2,1)} %get-tuple-element.43), calls=%async_computation.1 | async-start | bytes 786432 | tf_op jit(solution)/shard_map/all_to_all | solution.py:62
  48.8 0.0 copy-done
  48.9 0.0 copy-start.2
  48.9 1.3 copy-done.2
  50.1 2.9 %token_project.1 = (f32[32,768]{1,0:T(8,128)}, f32[32,768]{1,0:T(8,128)}, f32[32,768]{1,0:T(8,128)}, bf16[8,32,2304]{2,1,0:T(8,128)(2,1)}) custom-call(bf16[16,32,1024]{2,1,0:T(8,128)(2,1)S(1)} %all-to-all-done.parts, bf16[32,768]{1,0:T(8,128)(2,1)} %get-tuple-element.41.normed, bf16[768,128]{1,0:T(8,128)(2,1)} %wt2a.3, bf16[768,768]{1,0:T(8,128)(2,1)S(1)} %copy-done.2, ...), custom_call_target="tpu_custom_call" | custom-call | tf_op jit(solution)/shard_map/token_project/pallas_call | solution.py:137
  53.0 2.5 %all-to-all-done.1.keys = bf16[8,32,768]{2,1,0:T(8,128)(2,1)} async-done(((bf16[8,32,768]{2,1,0:T(8,128)(2,1)}), bf16[8,32,768]{2,1,0:T(8,128)(2,1)}, u32[]{:S(2)}, u32[]{:S(2)}) %all-to-all-start.1) | async-done | bytes 393248 | tf_op jit(solution)/shard_map/all_to_all | solution.py:62
  55.6 1.8 token_pack.1
  57.4 19.6 %all_to_all.40 = bf16[8,32,2304]{2,1,0:T(8,128)(2,1)S(1)} all-to-all(bf16[8,32,2304]{2,1,0:T(8,128)(2,1)} %token_pack.1), channel_id=1, replica_groups={{0,2,4,6,8,10,12,14},{1,3,5,7,9,11,13,15},{16,18,20,22,24,26,28,30},{17..., dimensions={0} | all-to-all | bytes 2359296 | tf_op jit(solution)/shard_map/all_to_all | solution.py:68
  77.0 2.7 %collective-permute-start.2 = (bf16[8,32,2304]{2,1,0:T(8,128)(2,1)S(1)}, bf16[8,32,2304]{2,1,0:T(8,128)(2,1)S(1)}, u32[]{:S(2)}, u32[]{:S(2)}) collective-permute-start(bf16[8,32,2304]{2,1,0:T(8,128)(2,1)S(1)} %all_to_all.40), channel_id=1, source_target_pairs={{0,1},{1,0},{2,3},{3,2},{4,5},{5,4},{6,7},{7,6},{8,9},{9,8},{10,11... | collective-permute-start | bytes 3538952 | tf_op jit(solution)/shard_map/ppermute | solution.py:74
  79.7 3.2 %token_keys.1 = (bf16[768,256]{1,0:T(8,128)(2,1)}, bf16[768,256]{1,0:T(8,128)(2,1)}) custom-call(bf16[256,2304]{1,0:T(8,128)(2,1)S(1)} %bitcast.18, bf16[768,1536]{1,0:T(8,128)(2,1)} %wv.3, bf16[768,1536]{1,0:T(8,128)(2,1)} %wv.3), custom_call_target="tpu_custom_call" | custom-call | tf_op jit(solution)/shard_map/token_keys/pallas_call | solution.py:189
  82.9 0.0 collective-permute-done.2
  82.9 8.6 %token_forward.1 = (bf16[512,768]{1,0:T(8,128)(2,1)}, bf16[768,512]{1,0:T(8,128)(2,1)}, bf16[512,768]{1,0:T(8,128)(2,1)}, bf16[768,512]{1,0:T(8,128)(2,1)}, bf16...) custom-call(s32[1]{0:T(128)} %bitcast.core, bf16[768,256]{1,0:T(8,128)(2,1)} %get-tuple-element.44.k_t, ...), custom_call_target="tpu_custom_call" | custom-call | tf_op jit(solution)/shard_map/token_forward/pallas_call | solution.py:266
  91.5 12.6 %all_to_all.41.mine = bf16[8,2,24,512]{3,2,1,0:T(8,128)(2,1)S(1)} all-to-all(bf16[8,2,24,512]{3,2,1,0:T(8,128)(2,1)} %get-tuple-element.46), channel_id=1, replica_groups={{0,2,4,6,8,10,12,14},{1,3,5,7,9,11,13,15},{16,18,20,22,24,26,28,30},{17..., dimensions={0} | all-to-all | bytes 786432 | tf_op jit(solution)/shard_map/all_to_all | solution.py:68
  104.1 6.4 %all-to-all-start.6 = ((bf16[16,32,768]{2,1,0:T(8,128)(2,1)}), bf16[16,32,768]{2,1,0:T(8,128)(2,1)S(1)}, u32[]{:S(2)}, u32[]{:S(2)}) async-start(bf16[16,32,768]{2,1,0:T(8,128)(2,1)} %get-tuple-element.54), calls=%async_computation.6 | async-start | bytes 1572864 | tf_op jit(solution)/shard_map/all_to_all | solution.py:62
  110.5 0.4 collective-permute-start.3
  110.9 1.4 collective-permute-done.3.theirs
  112.2 12.1 %token_backward.1 = (bf16[256,768]{1,0:T(8,128)(2,1)}, bf16[256,768]{1,0:T(8,128)(2,1)}, bf16[256,768]{1,0:T(8,128)(2,1)}) custom-call(s32[1]{0:T(128)} %bitcast.core, bf16[8,2,24,512]{3,2,1,0:T(8,128)(2,1)S(1)} %all_to_all.41.mine, bf16[8,2,24,512]{3,2,1,0:T(8,128)(2,1)S(1)} %collective-permute-done.3.theirs, bf16[512,768]{1,0:T(8,128)(2,1)} %get-tuple-element.47.q, ...), custom_call_target="tpu_custom_call" | custom-call | tf_op jit(solution)/shard_map/token_backward/pallas_call | solution.py:370
  124.3 0.4 collective-permute-start.4
  124.7 0.0 all-to-all-done.6.parts
  124.8 6.1 %all-to-all-start.5 = ((bf16[8,32,768]{2,1,0:T(8,128)(2,1)}), bf16[8,32,768]{2,1,0:T(8,128)(2,1)S(1)}, u32[]{:S(2)}, u32[]{:S(2)}) async-start(bf16[8,32,768]{2,1,0:T(8,128)(2,1)} %bitcast.30), calls=%async_computation.5 | async-start | bytes 786432 | tf_op jit(solution)/shard_map/all_to_all | solution.py:62
  130.9 0.0 collective-permute-done.4
  130.9 1.8 add_convert_fusion
  132.7 6.0 %all-to-all-done.5.parts = bf16[8,32,768]{2,1,0:T(8,128)(2,1)S(1)} async-done(((bf16[8,32,768]{2,1,0:T(8,128)(2,1)}), bf16[8,32,768]{2,1,0:T(8,128)(2,1)S(1)}, u32[]{:S(2)}, u32[]{:S(2)}) %all-to-all-start.5) | async-done | bytes 393248 | tf_op jit(solution)/shard_map/all_to_all | solution.py:62
  138.7 5.1 %all-to-all-start.4 = ((bf16[8,32,768]{2,1,0:T(8,128)(2,1)}), bf16[8,32,768]{2,1,0:T(8,128)(2,1)S(1)}, u32[]{:S(2)}, u32[]{:S(2)}) async-start(bf16[8,32,768]{2,1,0:T(8,128)(2,1)} %bitcast.10), calls=%async_computation.4 | async-start | bytes 786432 | tf_op jit(solution)/shard_map/all_to_all | solution.py:68
  143.7 0.1 token_keyval.1
  143.8 3.3 %collective-permute-start.5 = (bf16[32,768]{1,0:T(8,128)(2,1)S(1)}, bf16[32,768]{1,0:T(8,128)(2,1)S(1)}, u32[]{:S(2)}, u32[]{:S(2)}) collective-permute-start(bf16[32,768]{1,0:T(8,128)(2,1)S(1)} %token_keyval.1), channel_id=1, source_target_pairs={{0,0},{1,1},{16,2},{17,3},{32,4},{33,5},{48,6},{49,7},{64,8},{65,9... | collective-permute-start | bytes 147464 | tf_op jit(solution)/shard_map/ppermute | solution.py:831
  147.1 0.1 pad_add_fusion.1.place
  147.2 4.3 %token_own.1 = (bf16[32,768]{1,0:T(8,128)(2,1)S(1)}, bf16[32,128]{1,0:T(8,128)(2,1)S(1)}, f32[32,768]{1,0:T(8,128)S(1)}) custom-call(s32[2]{0:T(128)S(1)} %pad_add_fusion.1.place, bf16[16,32,768]{2,1,0:T(8,128)(2,1)S(1)} %all-to-all-done.6.parts, bf16[8,2,24,512]{3,2,1,0:T(8,128)(2,1)S(1)} %all_to_all.41.mine, ...), custom_call_target="tpu_custom_call" | custom-call | tf_op jit(solution)/shard_map/token_own/pallas_call | solution.py:435
  151.5 0.4 collective-permute-done.5.key_feature
  151.9 0.0 all-to-all-done.4.parts
  152.0 2.9 %token_grads.1 = bf16[8,32,992]{2,1,0:T(8,128)(2,1)} custom-call(bf16[8,32,768]{2,1,0:T(8,128)(2,1)S(1)} %all-to-all-done.4.parts, bf16[32,768]{1,0:T(8,128)(2,1)S(1)} %collective-permute-done.5.key_feature, f32[32,768]{1,0:T(8,128)S(1)} %get-tuple-element.58.feature, f32[32,768]{1,0:T(8,128)} %get-tuple-element.59.grad_new, ...), custom_call_target="tpu_custom_call" | custom-call | tf_op jit(solution)/shard_map/token_grads/pallas_call | solution.py:435
  154.8 11.3 %all_to_all.42 = bf16[8,32,992]{2,1,0:T(8,128)(2,1)S(1)} all-to-all(bf16[8,32,992]{2,1,0:T(8,128)(2,1)} %token_grads.1), channel_id=1, replica_groups={{0,2,4,6,8,10,12,14},{1,3,5,7,9,11,13,15},{16,18,20,22,24,26,28,30},{17..., dimensions={0} | all-to-all | bytes 1015808 | tf_op jit(solution)/shard_map/all_to_all | solution.py:68
  166.1 3.9 %collective-permute-start.6 = (bf16[8,32,992]{2,1,0:T(8,128)(2,1)S(1)}, bf16[8,32,992]{2,1,0:T(8,128)(2,1)S(1)}, u32[]{:S(2)}, u32[]{:S(2)}) collective-permute-start(bf16[8,32,992]{2,1,0:T(8,128)(2,1)S(1)} %all_to_all.42), channel_id=1, source_target_pairs={{0,1},{1,0},{2,3},{3,2},{4,5},{5,4},{6,7},{7,6},{8,9},{9,8},{10,11... | collective-permute-start | bytes 1523720 | tf_op jit(solution)/shard_map/ppermute | solution.py:74
  170.0 0.1 copy.29.token
  170.1 0.1 pad_add_fusion.place
  170.2 1.3 collective-permute-done.6
  171.5 0.0 copy-done.5
  171.5 5.6 %atoms_backward.1 = (bf16[256,128]{1,0:T(8,128)(2,1)}, bf16[512,48]{1,0:T(8,128)(2,1)S(1)}, bf16[512,48]{1,0:T(8,128)(2,1)S(1)}, f32[256,256]{1,0:T(8,128)}, bf1...) custom-call(s32[8]{0:T(128)S(1)} %subtract_add_fusion.starts, ...), custom_call_target="tpu_custom_call" | custom-call | tf_op jit(solution)/shard_map/atoms_backward/pallas_call | solution.py:435
  177.2 5.5 %collective-permute-start.7 = (bf16[64,256]{1,0:T(8,128)(2,1)S(1)}, bf16[64,256]{1,0:T(8,128)(2,1)S(1)}, u32[]{:S(2)}, u32[]{:S(2)}) collective-permute-start(bf16[64,256]{1,0:T(8,128)(2,1)S(1)} %get-tuple-element.71), channel_id=1, source_target_pairs={{0,1},{1,2},{2,3},{3,4},{4,5},{5,6},{6,7},{7,8},{8,9},{9,10},{10,1... | collective-permute-start | bytes 98312 | tf_op jit(solution)/shard_map/ppermute | solution.py:887
  182.7 1.9 collective-permute-start.8
  184.6 0.7 copy.30
  185.3 0.7 copy.31
  186.1 0.0 collective-permute-done.7.before
  186.1 6.1 %collective-permute-done.8.after = bf16[64,256]{1,0:T(8,128)(2,1)S(1)} collective-permute-done((bf16[64,256]{1,0:T(8,128)(2,1)S(1)}, bf16[64,256]{1,0:T(8,128)(2,1)S(1)}, u32[]{:S(2)}, u32[]{:S(2)}) %collective-permute-start.8) | collective-permute-done | bytes 32800 | tf_op jit(solution)/shard_map/ppermute | solution.py:888
  192.2 0.0 copy-done.7
  192.2 2.0 %atoms_last.1 = bf16[256,128]{1,0:T(8,128)(2,1)} custom-call(f32[256,256]{1,0:T(8,128)} %get-tuple-element.70.inner, bf16[64,256]{1,0:T(8,128)(2,1)S(1)} %collective-permute-done.7.before, bf16[64,256]{1,0:T(8,128)(2,1)S(1)} %collective-permute-done.8.after, f32[256,128]{1,0:T(8,128)} %get-tuple-element.73.feature, f32[256,128]{1,0:T(8,128)} %get-tuple-element.74.atoms_grad, ...), custom_call_target="tpu_custom_call" | custom-call | tf_op jit(solution)/shard_map/atoms_last/pallas_call | solution.py:435
  (12 shorter events, 0.0 us)
Async XLA Ops:
  1.4 7.0 %collective-permute-start = (bf16[64,128]{1,0:T(8,128)(2,1)S(1)}, bf16[64,128]{1,0:T(8,128)(2,1)S(1)}, u32[]{:S(2)}, u32[]{:S(2)}) collective-permute-start(bf16[64,128]{1,0:T(8,128)(2,1)S(1)} %get-tuple-element.85), channel_id=1, source_target_pairs={{0,1},{1,2},{2,3},{3,4},{4,5},{5,6},{6,7},{7,8},{8,9},{9,10},{10,1... | collective-permute-start | bytes 49160 | tf_op jit(solution)/shard_map/ppermute | solution.py:83
  5.0 9.3 %collective-permute-start.1 = (bf16[64,128]{1,0:T(8,128)(2,1)S(1)}, bf16[64,128]{1,0:T(8,128)(2,1)S(1)}, u32[]{:S(2)}, u32[]{:S(2)}) collective-permute-start(bf16[64,128]{1,0:T(8,128)(2,1)S(1)} %get-tuple-element.84), channel_id=1, source_target_pairs={{1,0},{2,1},{3,2},{4,3},{5,4},{6,5},{7,6},{8,7},{9,8},{10,9},{11,1... | collective-permute-start | bytes 49160 | tf_op jit(solution)/shard_map/ppermute | solution.py:84
  14.3 0.7 copy-start.6
  22.4 5.4 %copy-start.9 = (s32[512]{0:T(512)S(1)}, s32[512]{0:T(512)}, u32[]{:S(2)}) copy-start(s32[512]{0:T(512)} %param.25) | copy-start | bytes 6148
  22.4 5.6 %copy-start.8 = (f32[768]{0:T(1024)S(1)}, f32[768]{0:T(1024)}, u32[]{:S(2)}) copy-start(f32[768]{0:T(1024)} %param.32) | copy-start | bytes 9220
  22.5 26.4 %copy-start.1 = (bf16[768,768]{1,0:T(8,128)(2,1)S(1)}, bf16[768,768]{1,0:T(8,128)(2,1)}, u32[]{:S(2)}) copy-start(bf16[768,768]{1,0:T(8,128)(2,1)} %wout.3) | copy-start | bytes 3538948
  22.5 18.0 %all-to-all-start = ((bf16[16,32,1024]{2,1,0:T(8,128)(2,1)}), bf16[16,32,1024]{2,1,0:T(8,128)(2,1)S(1)}, u32[]{:S(2)}, u32[]{:S(2)}) async-start(bf16[16,32,1024]{2,1,0:T(8,128)(2,1)} %get-tuple-element.40), calls=%async_computation | async-start | bytes 2097152 | tf_op jit(solution)/shard_map/all_to_all | solution.py:62
  27.8 21.0 %copy-start = (bf16[768,768]{1,0:T(8,128)(2,1)S(1)}, bf16[768,768]{1,0:T(8,128)(2,1)}, u32[]{:S(2)}) copy-start(bf16[768,768]{1,0:T(8,128)(2,1)} %wgate.1) | copy-start | bytes 3538948
  41.6 14.0 %all-to-all-start.1 = ((bf16[8,32,768]{2,1,0:T(8,128)(2,1)}), bf16[8,32,768]{2,1,0:T(8,128)(2,1)}, u32[]{:S(2)}, u32[]{:S(2)}) async-start(bf16[8,32,768]{2,1,0:T(8,128)(2,1)} %get-tuple-element.43), calls=%async_computation.1 | async-start | bytes 786432 | tf_op jit(solution)/shard_map/all_to_all | solution.py:62
  48.9 1.3 copy-start.2
  77.0 5.9 %collective-permute-start.2 = (bf16[8,32,2304]{2,1,0:T(8,128)(2,1)S(1)}, bf16[8,32,2304]{2,1,0:T(8,128)(2,1)S(1)}, u32[]{:S(2)}, u32[]{:S(2)}) collective-permute-start(bf16[8,32,2304]{2,1,0:T(8,128)(2,1)S(1)} %all_to_all.40), channel_id=1, source_target_pairs={{0,1},{1,0},{2,3},{3,2},{4,5},{5,4},{6,7},{7,6},{8,9},{9,8},{10,11... | collective-permute-start | bytes 3538952 | tf_op jit(solution)/shard_map/ppermute | solution.py:74
  104.1 20.7 %all-to-all-start.6 = ((bf16[16,32,768]{2,1,0:T(8,128)(2,1)}), bf16[16,32,768]{2,1,0:T(8,128)(2,1)S(1)}, u32[]{:S(2)}, u32[]{:S(2)}) async-start(bf16[16,32,768]{2,1,0:T(8,128)(2,1)} %get-tuple-element.54), calls=%async_computation.6 | async-start | bytes 1572864 | tf_op jit(solution)/shard_map/all_to_all | solution.py:62
  110.5 1.7 collective-permute-start.3
  124.3 6.6 %collective-permute-start.4 = (bf16[256,768]{1,0:T(8,128)(2,1)}, bf16[256,768]{1,0:T(8,128)(2,1)S(1)}, u32[]{:S(2)}, u32[]{:S(2)}) collective-permute-start(bf16[256,768]{1,0:T(8,128)(2,1)} %get-tuple-element.52), channel_id=1, source_target_pairs={{0,1},{1,0},{2,3},{3,2},{4,5},{5,4},{6,7},{7,6},{8,9},{9,8},{10,11... | collective-permute-start | bytes 1179656 | tf_op jit(solution)/shard_map/ppermute | solution.py:803
  124.8 13.9 %all-to-all-start.5 = ((bf16[8,32,768]{2,1,0:T(8,128)(2,1)}), bf16[8,32,768]{2,1,0:T(8,128)(2,1)S(1)}, u32[]{:S(2)}, u32[]{:S(2)}) async-start(bf16[8,32,768]{2,1,0:T(8,128)(2,1)} %bitcast.30), calls=%async_computation.5 | async-start | bytes 786432 | tf_op jit(solution)/shard_map/all_to_all | solution.py:62
  138.7 13.3 %all-to-all-start.4 = ((bf16[8,32,768]{2,1,0:T(8,128)(2,1)}), bf16[8,32,768]{2,1,0:T(8,128)(2,1)S(1)}, u32[]{:S(2)}, u32[]{:S(2)}) async-start(bf16[8,32,768]{2,1,0:T(8,128)(2,1)} %bitcast.10), calls=%async_computation.4 | async-start | bytes 786432 | tf_op jit(solution)/shard_map/all_to_all | solution.py:68
  143.8 8.2 %collective-permute-start.5 = (bf16[32,768]{1,0:T(8,128)(2,1)S(1)}, bf16[32,768]{1,0:T(8,128)(2,1)S(1)}, u32[]{:S(2)}, u32[]{:S(2)}) collective-permute-start(bf16[32,768]{1,0:T(8,128)(2,1)S(1)} %token_keyval.1), channel_id=1, source_target_pairs={{0,0},{1,1},{16,2},{17,3},{32,4},{33,5},{48,6},{49,7},{64,8},{65,9... | collective-permute-start | bytes 147464 | tf_op jit(solution)/shard_map/ppermute | solution.py:831
  151.9 19.6 %copy-start.4 = (bf16[8,128,256]{2,1,0:T(8,128)(2,1)S(1)}, bf16[8,128,256]{2,1,0:T(8,128)(2,1)}, u32[]{:S(2)}) copy-start(bf16[8,128,256]{2,1,0:T(8,128)(2,1)} %get-tuple-element.65.window) | copy-start | bytes 1572868
  152.0 19.6 %copy-start.5 = (f32[8,128,128]{2,1,0:T(8,128)S(1)}, f32[8,128,128]{2,1,0:T(8,128)}, u32[]{:S(2)}) copy-start(f32[8,128,128]{2,1,0:T(8,128)} %get-tuple-element.66.prob) | copy-start | bytes 1572868
  154.8 16.7 %copy-start.3 = (f32[256,768]{1,0:T(8,128)S(1)}, f32[256,768]{1,0:T(8,128)}, u32[]{:S(2)}) copy-start(f32[256,768]{1,0:T(8,128)} %get-tuple-element.62.slope) | copy-start | bytes 2359300
  166.1 5.4 %collective-permute-start.6 = (bf16[8,32,992]{2,1,0:T(8,128)(2,1)S(1)}, bf16[8,32,992]{2,1,0:T(8,128)(2,1)S(1)}, u32[]{:S(2)}, u32[]{:S(2)}) collective-permute-start(bf16[8,32,992]{2,1,0:T(8,128)(2,1)S(1)} %all_to_all.42), channel_id=1, source_target_pairs={{0,1},{1,0},{2,3},{3,2},{4,5},{5,4},{6,7},{7,6},{8,9},{9,8},{10,11... | collective-permute-start | bytes 1523720 | tf_op jit(solution)/shard_map/ppermute | solution.py:74
  171.5 20.6 %copy-start.7 = (f32[128]{0:T(128)S(1)}, f32[128]{0:T(128)}, u32[]{:S(2)}) copy-start(f32[128]{0:T(128)} %param.27) | copy-start | bytes 1540
  177.2 8.9 %collective-permute-start.7 = (bf16[64,256]{1,0:T(8,128)(2,1)S(1)}, bf16[64,256]{1,0:T(8,128)(2,1)S(1)}, u32[]{:S(2)}, u32[]{:S(2)}) collective-permute-start(bf16[64,256]{1,0:T(8,128)(2,1)S(1)} %get-tuple-element.71), channel_id=1, source_target_pairs={{0,1},{1,2},{2,3},{3,4},{4,5},{5,6},{6,7},{7,8},{8,9},{9,10},{10,1... | collective-permute-start | bytes 98312 | tf_op jit(solution)/shard_map/ppermute | solution.py:887
  182.7 9.5 %collective-permute-start.8 = (bf16[64,256]{1,0:T(8,128)(2,1)S(1)}, bf16[64,256]{1,0:T(8,128)(2,1)S(1)}, u32[]{:S(2)}, u32[]{:S(2)}) collective-permute-start(bf16[64,256]{1,0:T(8,128)(2,1)S(1)} %get-tuple-element.72), channel_id=1, source_target_pairs={{1,0},{2,1},{3,2},{4,3},{5,4},{6,5},{7,6},{8,7},{9,8},{10,9},{11,1... | collective-permute-start | bytes 98312 | tf_op jit(solution)/shard_map/ppermute | solution.py:888
where the time goes:
time: 195 us; the launch traced here: 194 us
  starting transfers between devices  53.9 us (28%)
  Pallas kernels  52 us (27%)
  blocking collectives  43.5 us (22%)
  waiting for transfers between devices  36.1 us (19%)
  local copies, waits for them, and re-layouts  4.43 us (2%)
  other arithmetic  3.33 us (2%)
    all_to_all x3, blocking collectives, among_core(): return lax.all_to_all(x, 'col', 0, 0, axis_index_groups=groups)  43.5 us
    all_to_all x4, starting transfers between devices, exchange(): return lax.all_to_all(x, axis, 0, 0)  25.1 us
    pallas_call x7, Pallas kernels, whole(): pl.pallas_call(kernel, in_specs=specs, out_specs=[pl.BlockSpec(memory_spa...  23.5 us
    all_to_all x4, waiting for transfers between devices, exchange(): return lax.all_to_all(x, axis, 0, 0)  20.9 us
    pallas_call x1, Pallas kernels, token_backward(): pl.pallas_call(backward_kernel, grid=(groups,), in_specs=[pl.BlockSpec(me...  12.1 us
    pallas_call x1, Pallas kernels, token_forward(): pl.pallas_call(forward_kernel, grid=(groups,), in_specs=[pl.BlockSpec(mem...  8.57 us
    ppermute x3, starting transfers between devices, halves_of(): theirs = lax.ppermute(mine, 'col', [(i, i ^ 1) for i in range(cols)])  6.97 us
    ppermute x1, waiting for transfers between devices, local(): from_after = lax.ppermute(first, axes, down)  6.09 us
  transfers between devices with their start and end apart: 14, of which 8 were waited for; matrix products, arithmetic and copies ran while one was open for 3% of the time, Pallas kernels for 12%

commit v1 on v0

--- a/solution.py
+++ b/solution.py
@@ -468,7 +468,7 @@
 
 
 def atoms_forward_kernel(
-    starts, before, atoms, after, bias, token, gain, wq, wkv, wo, wagg, cot, tokens, tokens_cot,
+    starts, base, before, atoms, after, bias, token, gain, wq, wkv, wo, wagg, cot, tokens, tokens_cot,
     part, mid, slope, query, window, prob, mixed,
 ):
     atom_dev = atoms.shape[0]
@@ -483,7 +483,7 @@
     keyval = dot(normed, wkv[...]).astype(BF)
     for block in range(blocks):
         at = pl.ds(block * QBLK, QBLK)
-        rows = dot(picked(starts[block], padded_rows), keyval).astype(BF)
+        rows = dot(picked(starts[block] - base[0], padded_rows), keyval).astype(BF)
         window[block] = rows
         score = dot_t(stacked(query[at, :]), rows[:, :DA]) * scale + bias[block].astype(F32)
         exps = jnp.exp(score - jnp.max(score, axis=-1, keepdims=True))
@@ -492,7 +492,7 @@
         mixed[at, :] = unstacked(dot(one.astype(BF), rows[:, DA:])).astype(BF)
     mid[...] = (atoms[...].astype(F32) + dot(mixed[...], wo[...])).astype(BF)
     slot = lax.broadcasted_iota(jnp.int32, (tok_row, atom_dev), 0)
-    member = jnp.where(slot == token[...], 1.0, 0.0).astype(BF)
+    member = jnp.where(slot + base[1] == token[...], 1.0, 0.0).astype(BF)
     width = tokens.shape[0]
     cot_part = dot(member, cot[...]).astype(BF)
     blank = jnp.zeros((part.shape[2] - D - DA - 2 * width, tok_row), BF)
@@ -742,13 +742,14 @@
             pltpu.HBM((atom_dev, DA), BF),
         ],
         (
-            starts,
+            window_starts,
+            jnp.stack([first_atom - RIM, row_index * tok_row]),
             before,
             far(atoms),
             after,
             far(atom_bias.reshape(blocks, AH * QBLK, KWIN)),
-            local_token[None, :],
-            gain_a,
+            far(atom_index[None, :]),
+            far(gain_a),
             far(w_atom_q),
             far(w_atom_kv),
             far(w_atom_o),
@@ -758,7 +759,7 @@
             far(tokens_cot.T),
         ),
         "atoms_forward",
-        scalars=1,
+        scalars=2,
     )
 
     sums = exchange(part, "col")

time: 195 us -> 196 us (level)
  transfers between devices with their start and end apart: 14 -> 14, of which waited for: 8 -> 8; matrix products, arithmetic and copies ran while one was open for 3% -> 2% of each run, Pallas kernels for 12% -> 12%
where the time goes in v1:
time: 196 us; the launch traced here: 194 us
  starting transfers between devices  54 us (28%)
  Pallas kernels  52.2 us (27%)
  blocking collectives  43.5 us (22%)
  waiting for transfers between devices  37.3 us (19%)
  local copies, waits for them, and re-layouts  4.44 us (2%)
  other arithmetic  2.1 us (1%)
    all_to_all x3, blocking collectives, among_core(): return lax.all_to_all(x, 'col', 0, 0, axis_index_groups=groups)  43.5 us
    all_to_all x4, starting transfers between devices, exchange(): return lax.all_to_all(x, axis, 0, 0)  25.1 us
    pallas_call x7, Pallas kernels, whole(): pl.pallas_call(kernel, in_specs=specs, out_specs=[pl.BlockSpec(memory_spa...  23.5 us
    all_to_all x4, waiting for transfers between devices, exchange(): return lax.all_to_all(x, axis, 0, 0)  20.9 us
    pallas_call x1, Pallas kernels, token_backward(): pl.pallas_call(backward_kernel, grid=(groups,), in_specs=[pl.BlockSpec(me...  12.1 us
    pallas_call x1, Pallas kernels, token_forward(): pl.pallas_call(forward_kernel, grid=(groups,), in_specs=[pl.BlockSpec(mem...  8.62 us
    ppermute x1, waiting for transfers between devices, neighbours(): after = lax.ppermute(x[:width], axes, down)  7.26 us
    ppermute x3, starting transfers between devices, halves_of(): theirs = lax.ppermute(mine, 'col', [(i, i ^ 1) for i in range(cols)])  6.97 us
  transfers between devices with their start and end apart: 14, of which 8 were waited for; matrix products, arithmetic and copies ran while one was open for 2% of the time, Pallas kernels for 12%

profile of v1, /device:TPU:31, one launch (start us, length us, event | category | flops | bytes accessed | tf_op | source)
XLA Modules:
  0.0 194.3 jit_solution(3674294966538589606)
XLA Ops:
  0.6 0.7 fusion
  1.4 3.7 %collective-permute-start = (bf16[64,128]{1,0:T(8,128)(2,1)S(1)}, bf16[64,128]{1,0:T(8,128)(2,1)S(1)}, u32[]{:S(2)}, u32[]{:S(2)}) collective-permute-start(bf16[64,128]{1,0:T(8,128)(2,1)S(1)} %get-tuple-element.85), channel_id=1, source_target_pairs={{0,1},{1,2},{2,3},{3,4},{4,5},{5,6},{6,7},{7,8},{8,9},{9,10},{10,1... | collective-permute-start | bytes 49160 | tf_op jit(solution)/shard_map/ppermute | solution.py:83
  5.0 1.9 collective-permute-start.1
  7.0 0.1 pad_add_fusion.1.base
  7.1 0.0 collective-permute-done.before
  7.1 7.3 %collective-permute-done.1.after = bf16[64,128]{1,0:T(8,128)(2,1)S(1)} collective-permute-done((bf16[64,128]{1,0:T(8,128)(2,1)S(1)}, bf16[64,128]{1,0:T(8,128)(2,1)S(1)}, u32[]{:S(2)}, u32[]{:S(2)}) %collective-permute-start.1) | collective-permute-done | bytes 16416 | tf_op jit(solution)/shard_map/ppermute | solution.py:84
  14.3 0.7 copy-done.7
  15.0 7.5 %atoms_forward.1 = (bf16[16,32,1024]{2,1,0:T(8,128)(2,1)}, bf16[256,128]{1,0:T(8,128)(2,1)}, f32[256,768]{1,0:T(8,128)}, bf16[256,128]{1,0:T(8,128)(2,1)}, bf16[...) custom-call(s32[8]{0:T(128)S(1)} %copy-done.7, s32[2]{0:T(128)S(1)} %pad_add_fusion.1.base, ...), custom_call_target="tpu_custom_call" | custom-call | tf_op jit(solution)/shard_map/atoms_forward/pallas_call | solution.py:435
  22.5 0.0 copy-start.11
  22.5 0.0 copy-start.10
  22.5 0.0 copy-start.1
  22.5 5.3 %all-to-all-start = ((bf16[16,32,1024]{2,1,0:T(8,128)(2,1)}), bf16[16,32,1024]{2,1,0:T(8,128)(2,1)S(1)}, u32[]{:S(2)}, u32[]{:S(2)}) async-start(bf16[16,32,1024]{2,1,0:T(8,128)(2,1)} %get-tuple-element.40), calls=%async_computation | async-start | bytes 2097152 | tf_op jit(solution)/shard_map/all_to_all | solution.py:62
  27.9 0.0 copy-done.11
  27.9 0.1 dynamic-slice_bitcast_fusion
  28.0 0.1 copy.28.inverse
  28.1 0.0 copy-done.10
  28.1 12.4 %all-to-all-done.parts = bf16[16,32,1024]{2,1,0:T(8,128)(2,1)S(1)} async-done(((bf16[16,32,1024]{2,1,0:T(8,128)(2,1)}), bf16[16,32,1024]{2,1,0:T(8,128)(2,1)S(1)}, u32[]{:S(2)}, u32[]{:S(2)}) %all-to-all-start) | async-done | bytes 1048608 | tf_op jit(solution)/shard_map/all_to_all | solution.py:62
  40.5 1.1 token_norm.1
  41.6 7.3 %all-to-all-start.1 = ((bf16[8,32,768]{2,1,0:T(8,128)(2,1)}), bf16[8,32,768]{2,1,0:T(8,128)(2,1)}, u32[]{:S(2)}, u32[]{:S(2)}) async-start(bf16[8,32,768]{2,1,0:T(8,128)(2,1)} %get-tuple-element.43), calls=%async_computation.1 | async-start | bytes 786432 | tf_op jit(solution)/shard_map/all_to_all | solution.py:62
  48.9 0.0 copy-start.2
  48.9 1.3 copy-done.2
  50.2 2.9 %token_project.1 = (f32[32,768]{1,0:T(8,128)}, f32[32,768]{1,0:T(8,128)}, f32[32,768]{1,0:T(8,128)}, bf16[8,32,2304]{2,1,0:T(8,128)(2,1)}) custom-call(bf16[16,32,1024]{2,1,0:T(8,128)(2,1)S(1)} %all-to-all-done.parts, bf16[32,768]{1,0:T(8,128)(2,1)} %get-tuple-element.41.normed, bf16[768,128]{1,0:T(8,128)(2,1)} %wt2a.3, bf16[768,768]{1,0:T(8,128)(2,1)S(1)} %copy-done.2, ...), custom_call_target="tpu_custom_call" | custom-call | tf_op jit(solution)/shard_map/token_project/pallas_call | solution.py:137
  53.1 2.5 %all-to-all-done.1.keys = bf16[8,32,768]{2,1,0:T(8,128)(2,1)} async-done(((bf16[8,32,768]{2,1,0:T(8,128)(2,1)}), bf16[8,32,768]{2,1,0:T(8,128)(2,1)}, u32[]{:S(2)}, u32[]{:S(2)}) %all-to-all-start.1) | async-done | bytes 393248 | tf_op jit(solution)/shard_map/all_to_all | solution.py:62
  55.6 1.8 token_pack.1
  57.4 19.6 %all_to_all.40 = bf16[8,32,2304]{2,1,0:T(8,128)(2,1)S(1)} all-to-all(bf16[8,32,2304]{2,1,0:T(8,128)(2,1)} %token_pack.1), channel_id=1, replica_groups={{0,2,4,6,8,10,12,14},{1,3,5,7,9,11,13,15},{16,18,20,22,24,26,28,30},{17..., dimensions={0} | all-to-all | bytes 2359296 | tf_op jit(solution)/shard_map/all_to_all | solution.py:68
  77.0 2.7 %collective-permute-start.2 = (bf16[8,32,2304]{2,1,0:T(8,128)(2,1)S(1)}, bf16[8,32,2304]{2,1,0:T(8,128)(2,1)S(1)}, u32[]{:S(2)}, u32[]{:S(2)}) collective-permute-start(bf16[8,32,2304]{2,1,0:T(8,128)(2,1)S(1)} %all_to_all.40), channel_id=1, source_target_pairs={{0,1},{1,0},{2,3},{3,2},{4,5},{5,4},{6,7},{7,6},{8,9},{9,8},{10,11... | collective-permute-start | bytes 3538952 | tf_op jit(solution)/shard_map/ppermute | solution.py:74
  79.8 3.2 %token_keys.1 = (bf16[768,256]{1,0:T(8,128)(2,1)}, bf16[768,256]{1,0:T(8,128)(2,1)}) custom-call(bf16[256,2304]{1,0:T(8,128)(2,1)S(1)} %bitcast.20, bf16[768,1536]{1,0:T(8,128)(2,1)} %wv.3, bf16[768,1536]{1,0:T(8,128)(2,1)} %wv.3), custom_call_target="tpu_custom_call" | custom-call | tf_op jit(solution)/shard_map/token_keys/pallas_call | solution.py:189
  83.0 0.0 collective-permute-done.2
  83.0 8.6 %token_forward.1 = (bf16[512,768]{1,0:T(8,128)(2,1)}, bf16[768,512]{1,0:T(8,128)(2,1)}, bf16[512,768]{1,0:T(8,128)(2,1)}, bf16[768,512]{1,0:T(8,128)(2,1)}, bf16...) custom-call(s32[1]{0:T(128)} %bitcast.core, bf16[768,256]{1,0:T(8,128)(2,1)} %get-tuple-element.44.k_t, ...), custom_call_target="tpu_custom_call" | custom-call | tf_op jit(solution)/shard_map/token_forward/pallas_call | solution.py:266
  91.6 12.6 %all_to_all.41.mine = bf16[8,2,24,512]{3,2,1,0:T(8,128)(2,1)S(1)} all-to-all(bf16[8,2,24,512]{3,2,1,0:T(8,128)(2,1)} %get-tuple-element.46), channel_id=1, replica_groups={{0,2,4,6,8,10,12,14},{1,3,5,7,9,11,13,15},{16,18,20,22,24,26,28,30},{17..., dimensions={0} | all-to-all | bytes 786432 | tf_op jit(solution)/shard_map/all_to_all | solution.py:68
  104.2 6.4 %all-to-all-start.6 = ((bf16[16,32,768]{2,1,0:T(8,128)(2,1)}), bf16[16,32,768]{2,1,0:T(8,128)(2,1)S(1)}, u32[]{:S(2)}, u32[]{:S(2)}) async-start(bf16[16,32,768]{2,1,0:T(8,128)(2,1)} %get-tuple-element.54), calls=%async_computation.6 | async-start | bytes 1572864 | tf_op jit(solution)/shard_map/all_to_all | solution.py:62
  110.6 0.4 collective-permute-start.3
  110.9 1.4 collective-permute-done.3.theirs
  112.3 12.1 %token_backward.1 = (bf16[256,768]{1,0:T(8,128)(2,1)}, bf16[256,768]{1,0:T(8,128)(2,1)}, bf16[256,768]{1,0:T(8,128)(2,1)}) custom-call(s32[1]{0:T(128)} %bitcast.core, bf16[8,2,24,512]{3,2,1,0:T(8,128)(2,1)S(1)} %all_to_all.41.mine, bf16[8,2,24,512]{3,2,1,0:T(8,128)(2,1)S(1)} %collective-permute-done.3.theirs, bf16[512,768]{1,0:T(8,128)(2,1)} %get-tuple-element.47.q, ...), custom_call_target="tpu_custom_call" | custom-call | tf_op jit(solution)/shard_map/token_backward/pallas_call | solution.py:370
  124.4 0.4 collective-permute-start.4
  124.8 0.0 all-to-all-done.6.parts
  124.8 6.1 %all-to-all-start.5 = ((bf16[8,32,768]{2,1,0:T(8,128)(2,1)}), bf16[8,32,768]{2,1,0:T(8,128)(2,1)S(1)}, u32[]{:S(2)}, u32[]{:S(2)}) async-start(bf16[8,32,768]{2,1,0:T(8,128)(2,1)} %bitcast.30), calls=%async_computation.5 | async-start | bytes 786432 | tf_op jit(solution)/shard_map/all_to_all | solution.py:62
  131.0 0.0 collective-permute-done.4
  131.0 1.9 add_convert_fusion
  132.8 5.9 %all-to-all-done.5.parts = bf16[8,32,768]{2,1,0:T(8,128)(2,1)S(1)} async-done(((bf16[8,32,768]{2,1,0:T(8,128)(2,1)}), bf16[8,32,768]{2,1,0:T(8,128)(2,1)S(1)}, u32[]{:S(2)}, u32[]{:S(2)}) %all-to-all-start.5) | async-done | bytes 393248 | tf_op jit(solution)/shard_map/all_to_all | solution.py:62
  138.7 5.1 %all-to-all-start.4 = ((bf16[8,32,768]{2,1,0:T(8,128)(2,1)}), bf16[8,32,768]{2,1,0:T(8,128)(2,1)S(1)}, u32[]{:S(2)}, u32[]{:S(2)}) async-start(bf16[8,32,768]{2,1,0:T(8,128)(2,1)} %bitcast.12), calls=%async_computation.4 | async-start | bytes 786432 | tf_op jit(solution)/shard_map/all_to_all | solution.py:68
  143.8 0.1 token_keyval.1
  143.9 3.3 %collective-permute-start.5 = (bf16[32,768]{1,0:T(8,128)(2,1)S(1)}, bf16[32,768]{1,0:T(8,128)(2,1)S(1)}, u32[]{:S(2)}, u32[]{:S(2)}) collective-permute-start(bf16[32,768]{1,0:T(8,128)(2,1)S(1)} %token_keyval.1), channel_id=1, source_target_pairs={{0,0},{1,1},{16,2},{17,3},{32,4},{33,5},{48,6},{49,7},{64,8},{65,9... | collective-permute-start | bytes 147464 | tf_op jit(solution)/shard_map/ppermute | solution.py:832
  147.2 0.1 pad_add_fusion.2.place
  147.3 4.3 %token_own.1 = (bf16[32,768]{1,0:T(8,128)(2,1)S(1)}, bf16[32,128]{1,0:T(8,128)(2,1)S(1)}, f32[32,768]{1,0:T(8,128)S(1)}) custom-call(s32[2]{0:T(128)S(1)} %pad_add_fusion.2.place, bf16[16,32,768]{2,1,0:T(8,128)(2,1)S(1)} %all-to-all-done.6.parts, bf16[8,2,24,512]{3,2,1,0:T(8,128)(2,1)S(1)} %all_to_all.41.mine, ...), custom_call_target="tpu_custom_call" | custom-call | tf_op jit(solution)/shard_map/token_own/pallas_call | solution.py:435
  151.6 0.4 collective-permute-done.5.key_feature
  152.0 0.0 all-to-all-done.4.parts
  152.1 2.9 %token_grads.1 = bf16[8,32,992]{2,1,0:T(8,128)(2,1)} custom-call(bf16[8,32,768]{2,1,0:T(8,128)(2,1)S(1)} %all-to-all-done.4.parts, bf16[32,768]{1,0:T(8,128)(2,1)S(1)} %collective-permute-done.5.key_feature, f32[32,768]{1,0:T(8,128)S(1)} %get-tuple-element.58.feature, f32[32,768]{1,0:T(8,128)} %get-tuple-element.59.grad_new, ...), custom_call_target="tpu_custom_call" | custom-call | tf_op jit(solution)/shard_map/token_grads/pallas_call | solution.py:435
  154.9 11.3 %all_to_all.42 = bf16[8,32,992]{2,1,0:T(8,128)(2,1)S(1)} all-to-all(bf16[8,32,992]{2,1,0:T(8,128)(2,1)} %token_grads.1), channel_id=1, replica_groups={{0,2,4,6,8,10,12,14},{1,3,5,7,9,11,13,15},{16,18,20,22,24,26,28,30},{17..., dimensions={0} | all-to-all | bytes 1015808 | tf_op jit(solution)/shard_map/all_to_all | solution.py:68
  166.2 3.9 %collective-permute-start.6 = (bf16[8,32,992]{2,1,0:T(8,128)(2,1)S(1)}, bf16[8,32,992]{2,1,0:T(8,128)(2,1)S(1)}, u32[]{:S(2)}, u32[]{:S(2)}) collective-permute-start(bf16[8,32,992]{2,1,0:T(8,128)(2,1)S(1)} %all_to_all.42), channel_id=1, source_target_pairs={{0,1},{1,0},{2,3},{3,2},{4,5},{5,4},{6,7},{7,6},{8,9},{9,8},{10,11... | collective-permute-start | bytes 1523720 | tf_op jit(solution)/shard_map/ppermute | solution.py:74
  170.1 0.0 copy-done.9
  170.1 0.1 copy.29.token
  170.2 0.1 pad_add_fusion.place
  170.3 1.3 collective-permute-done.6
  171.6 0.0 copy-done.5
  171.6 5.6 %atoms_backward.1 = (bf16[256,128]{1,0:T(8,128)(2,1)}, bf16[512,48]{1,0:T(8,128)(2,1)S(1)}, bf16[512,48]{1,0:T(8,128)(2,1)S(1)}, f32[256,256]{1,0:T(8,128)}, bf1...) custom-call(s32[8]{0:T(128)S(1)} %subtract_add_fusion.starts, ...), custom_call_target="tpu_custom_call" | custom-call | tf_op jit(solution)/shard_map/atoms_backward/pallas_call | solution.py:435
  177.3 5.5 %collective-permute-start.7 = (bf16[64,256]{1,0:T(8,128)(2,1)S(1)}, bf16[64,256]{1,0:T(8,128)(2,1)S(1)}, u32[]{:S(2)}, u32[]{:S(2)}) collective-permute-start(bf16[64,256]{1,0:T(8,128)(2,1)S(1)} %get-tuple-element.71), channel_id=1, source_target_pairs={{0,1},{1,2},{2,3},{3,4},{4,5},{5,6},{6,7},{7,8},{8,9},{9,10},{10,1... | collective-permute-start | bytes 98312 | tf_op jit(solution)/shard_map/ppermute | solution.py:888
  182.8 1.9 collective-permute-start.8
  184.8 0.7 copy.30
  185.5 0.7 copy.31
  186.2 0.0 collective-permute-done.7.before
  186.2 6.1 %collective-permute-done.8.after = bf16[64,256]{1,0:T(8,128)(2,1)S(1)} collective-permute-done((bf16[64,256]{1,0:T(8,128)(2,1)S(1)}, bf16[64,256]{1,0:T(8,128)(2,1)S(1)}, u32[]{:S(2)}, u32[]{:S(2)}) %collective-permute-start.8) | collective-permute-done | bytes 32800 | tf_op jit(solution)/shard_map/ppermute | solution.py:889
  192.3 0.0 copy-done.6
  192.3 2.0 %atoms_last.1 = bf16[256,128]{1,0:T(8,128)(2,1)} custom-call(f32[256,256]{1,0:T(8,128)} %get-tuple-element.70.inner, bf16[64,256]{1,0:T(8,128)(2,1)S(1)} %collective-permute-done.7.before, bf16[64,256]{1,0:T(8,128)(2,1)S(1)} %collective-permute-done.8.after, f32[256,128]{1,0:T(8,128)} %get-tuple-element.73.feature, f32[256,128]{1,0:T(8,128)} %get-tuple-element.74.atoms_grad, ...), custom_call_target="tpu_custom_call" | custom-call | tf_op jit(solution)/shard_map/atoms_last/pallas_call | solution.py:435
  (17 shorter events, 0.0 us)
Async XLA Ops:
  1.4 5.7 %collective-permute-start = (bf16[64,128]{1,0:T(8,128)(2,1)S(1)}, bf16[64,128]{1,0:T(8,128)(2,1)S(1)}, u32[]{:S(2)}, u32[]{:S(2)}) collective-permute-start(bf16[64,128]{1,0:T(8,128)(2,1)S(1)} %get-tuple-element.85), channel_id=1, source_target_pairs={{0,1},{1,2},{2,3},{3,4},{4,5},{5,6},{6,7},{7,8},{8,9},{9,10},{10,1... | collective-permute-start | bytes 49160 | tf_op jit(solution)/shard_map/ppermute | solution.py:83
  5.0 9.3 %collective-permute-start.1 = (bf16[64,128]{1,0:T(8,128)(2,1)S(1)}, bf16[64,128]{1,0:T(8,128)(2,1)S(1)}, u32[]{:S(2)}, u32[]{:S(2)}) collective-permute-start(bf16[64,128]{1,0:T(8,128)(2,1)S(1)} %get-tuple-element.84), channel_id=1, source_target_pairs={{1,0},{2,1},{3,2},{4,3},{5,4},{6,5},{7,6},{8,7},{9,8},{10,9},{11,1... | collective-permute-start | bytes 49160 | tf_op jit(solution)/shard_map/ppermute | solution.py:84
  14.3 0.7 copy-start.7
  22.5 5.4 %copy-start.11 = (s32[512]{0:T(512)S(1)}, s32[512]{0:T(512)}, u32[]{:S(2)}) copy-start(s32[512]{0:T(512)} %param.25) | copy-start | bytes 6148
  22.5 5.6 %copy-start.10 = (f32[768]{0:T(1024)S(1)}, f32[768]{0:T(1024)}, u32[]{:S(2)}) copy-start(f32[768]{0:T(1024)} %param.32) | copy-start | bytes 9220
  22.5 26.4 %copy-start.1 = (bf16[768,768]{1,0:T(8,128)(2,1)S(1)}, bf16[768,768]{1,0:T(8,128)(2,1)}, u32[]{:S(2)}) copy-start(bf16[768,768]{1,0:T(8,128)(2,1)} %wout.3) | copy-start | bytes 3538948
  22.5 18.0 %all-to-all-start = ((bf16[16,32,1024]{2,1,0:T(8,128)(2,1)}), bf16[16,32,1024]{2,1,0:T(8,128)(2,1)S(1)}, u32[]{:S(2)}, u32[]{:S(2)}) async-start(bf16[16,32,1024]{2,1,0:T(8,128)(2,1)} %get-tuple-element.40), calls=%async_computation | async-start | bytes 2097152 | tf_op jit(solution)/shard_map/all_to_all | solution.py:62
  27.8 21.1 %copy-start = (bf16[768,768]{1,0:T(8,128)(2,1)S(1)}, bf16[768,768]{1,0:T(8,128)(2,1)}, u32[]{:S(2)}) copy-start(bf16[768,768]{1,0:T(8,128)(2,1)} %wgate.1) | copy-start | bytes 3538948
  41.6 14.0 %all-to-all-start.1 = ((bf16[8,32,768]{2,1,0:T(8,128)(2,1)}), bf16[8,32,768]{2,1,0:T(8,128)(2,1)}, u32[]{:S(2)}, u32[]{:S(2)}) async-start(bf16[8,32,768]{2,1,0:T(8,128)(2,1)} %get-tuple-element.43), calls=%async_computation.1 | async-start | bytes 786432 | tf_op jit(solution)/shard_map/all_to_all | solution.py:62
  48.9 1.3 copy-start.2
  77.0 5.9 %collective-permute-start.2 = (bf16[8,32,2304]{2,1,0:T(8,128)(2,1)S(1)}, bf16[8,32,2304]{2,1,0:T(8,128)(2,1)S(1)}, u32[]{:S(2)}, u32[]{:S(2)}) collective-permute-start(bf16[8,32,2304]{2,1,0:T(8,128)(2,1)S(1)} %all_to_all.40), channel_id=1, source_target_pairs={{0,1},{1,0},{2,3},{3,2},{4,5},{5,4},{6,7},{7,6},{8,9},{9,8},{10,11... | collective-permute-start | bytes 3538952 | tf_op jit(solution)/shard_map/ppermute | solution.py:74
  104.2 20.7 %all-to-all-start.6 = ((bf16[16,32,768]{2,1,0:T(8,128)(2,1)}), bf16[16,32,768]{2,1,0:T(8,128)(2,1)S(1)}, u32[]{:S(2)}, u32[]{:S(2)}) async-start(bf16[16,32,768]{2,1,0:T(8,128)(2,1)} %get-tuple-element.54), calls=%async_computation.6 | async-start | bytes 1572864 | tf_op jit(solution)/shard_map/all_to_all | solution.py:62
  110.6 1.7 collective-permute-start.3
  124.4 6.5 %collective-permute-start.4 = (bf16[256,768]{1,0:T(8,128)(2,1)}, bf16[256,768]{1,0:T(8,128)(2,1)S(1)}, u32[]{:S(2)}, u32[]{:S(2)}) collective-permute-start(bf16[256,768]{1,0:T(8,128)(2,1)} %get-tuple-element.52), channel_id=1, source_target_pairs={{0,1},{1,0},{2,3},{3,2},{4,5},{5,4},{6,7},{7,6},{8,9},{9,8},{10,11... | collective-permute-start | bytes 1179656 | tf_op jit(solution)/shard_map/ppermute | solution.py:804
  124.8 13.9 %all-to-all-start.5 = ((bf16[8,32,768]{2,1,0:T(8,128)(2,1)}), bf16[8,32,768]{2,1,0:T(8,128)(2,1)S(1)}, u32[]{:S(2)}, u32[]{:S(2)}) async-start(bf16[8,32,768]{2,1,0:T(8,128)(2,1)} %bitcast.30), calls=%async_computation.5 | async-start | bytes 786432 | tf_op jit(solution)/shard_map/all_to_all | solution.py:62
  138.7 13.3 %all-to-all-start.4 = ((bf16[8,32,768]{2,1,0:T(8,128)(2,1)}), bf16[8,32,768]{2,1,0:T(8,128)(2,1)S(1)}, u32[]{:S(2)}, u32[]{:S(2)}) async-start(bf16[8,32,768]{2,1,0:T(8,128)(2,1)} %bitcast.12), calls=%async_computation.4 | async-start | bytes 786432 | tf_op jit(solution)/shard_map/all_to_all | solution.py:68
  143.9 8.2 %collective-permute-start.5 = (bf16[32,768]{1,0:T(8,128)(2,1)S(1)}, bf16[32,768]{1,0:T(8,128)(2,1)S(1)}, u32[]{:S(2)}, u32[]{:S(2)}) collective-permute-start(bf16[32,768]{1,0:T(8,128)(2,1)S(1)} %token_keyval.1), channel_id=1, source_target_pairs={{0,0},{1,1},{16,2},{17,3},{32,4},{33,5},{48,6},{49,7},{64,8},{65,9... | collective-permute-start | bytes 147464 | tf_op jit(solution)/shard_map/ppermute | solution.py:832
  152.0 18.1 %copy-start.9 = (s32[256]{0:T(256)S(1)}, s32[256]{0:T(256)}, u32[]{:S(2)}) copy-start(s32[256]{0:T(256)} %param.24) | copy-start | bytes 3076
  152.0 19.6 %copy-start.4 = (bf16[8,128,256]{2,1,0:T(8,128)(2,1)S(1)}, bf16[8,128,256]{2,1,0:T(8,128)(2,1)}, u32[]{:S(2)}) copy-start(bf16[8,128,256]{2,1,0:T(8,128)(2,1)} %get-tuple-element.65.window) | copy-start | bytes 1572868
  152.0 19.6 %copy-start.5 = (f32[8,128,128]{2,1,0:T(8,128)S(1)}, f32[8,128,128]{2,1,0:T(8,128)}, u32[]{:S(2)}) copy-start(f32[8,128,128]{2,1,0:T(8,128)} %get-tuple-element.66.prob) | copy-start | bytes 1572868
  154.9 15.4 %copy-start.8 = (s32[8]{0:T(128)S(1)}, s32[8]{0:T(128)}, u32[]{:S(2)}) copy-start(s32[8]{0:T(128)} %starts.1) | copy-start | bytes 100
  154.9 16.7 %copy-start.3 = (f32[256,768]{1,0:T(8,128)S(1)}, f32[256,768]{1,0:T(8,128)}, u32[]{:S(2)}) copy-start(f32[256,768]{1,0:T(8,128)} %get-tuple-element.62.slope) | copy-start | bytes 2359300
  166.2 5.4 %collective-permute-start.6 = (bf16[8,32,992]{2,1,0:T(8,128)(2,1)S(1)}, bf16[8,32,992]{2,1,0:T(8,128)(2,1)S(1)}, u32[]{:S(2)}, u32[]{:S(2)}) collective-permute-start(bf16[8,32,992]{2,1,0:T(8,128)(2,1)S(1)} %all_to_all.42), channel_id=1, source_target_pairs={{0,1},{1,0},{2,3},{3,2},{4,5},{5,4},{6,7},{7,6},{8,9},{9,8},{10,11... | collective-permute-start | bytes 1523720 | tf_op jit(solution)/shard_map/ppermute | solution.py:74
  171.6 20.6 %copy-start.6 = (f32[128]{0:T(128)S(1)}, f32[128]{0:T(128)}, u32[]{:S(2)}) copy-start(f32[128]{0:T(128)} %param.27) | copy-start | bytes 1540
  177.3 8.9 %collective-permute-start.7 = (bf16[64,256]{1,0:T(8,128)(2,1)S(1)}, bf16[64,256]{1,0:T(8,128)(2,1)S(1)}, u32[]{:S(2)}, u32[]{:S(2)}) collective-permute-start(bf16[64,256]{1,0:T(8,128)(2,1)S(1)} %get-tuple-element.71), channel_id=1, source_target_pairs={{0,1},{1,2},{2,3},{3,4},{4,5},{5,6},{6,7},{7,8},{8,9},{9,10},{10,1... | collective-permute-start | bytes 98312 | tf_op jit(solution)/shard_map/ppermute | solution.py:888
  182.8 9.5 %collective-permute-start.8 = (bf16[64,256]{1,0:T(8,128)(2,1)S(1)}, bf16[64,256]{1,0:T(8,128)(2,1)S(1)}, u32[]{:S(2)}, u32[]{:S(2)}) collective-permute-start(bf16[64,256]{1,0:T(8,128)(2,1)S(1)} %get-tuple-element.72), channel_id=1, source_target_pairs={{1,0},{2,1},{3,2},{4,3},{5,4},{6,5},{7,6},{8,7},{9,8},{10,9},{11,1... | collective-permute-start | bytes 98312 | tf_op jit(solution)/shard_map/ppermute | solution.py:889

commit v2 on v0

--- a/solution.py
+++ b/solution.py
@@ -295,7 +295,7 @@
         scratch_shapes=[pltpu.VMEM((rows, tok_col), BF), pltpu.VMEM((span, rows), F32)],
         compiler_params=pltpu.CompilerParams(vmem_limit_bytes=VMEM_LIMIT),
         name="token_forward",
-    )(core, far(k_t), far(v_t), mine, theirs, mine, theirs, far(bias))
+    )(core, far(k_t), far(v_t), mine, theirs, mine, theirs, bias)
 
 
 def backward_kernel(

time: 195 us -> 195 us (level)
  no operation moved by 1% of the time
where the time goes in v2:
time: 195 us; the launch traced here: 194 us
  starting transfers between devices  54 us (28%)
  Pallas kernels  51.5 us (26%)
  blocking collectives  43.5 us (22%)
  waiting for transfers between devices  36.1 us (19%)
  local copies, waits for them, and re-layouts  4.43 us (2%)
  other arithmetic  3.34 us (2%)
    all_to_all x3, blocking collectives, among_core(): return lax.all_to_all(x, 'col', 0, 0, axis_index_groups=groups)  43.5 us
    all_to_all x4, starting transfers between devices, exchange(): return lax.all_to_all(x, axis, 0, 0)  25.1 us
    pallas_call x7, Pallas kernels, whole(): pl.pallas_call(kernel, in_specs=specs, out_specs=[pl.BlockSpec(memory_spa...  23.5 us
    all_to_all x4, waiting for transfers between devices, exchange(): return lax.all_to_all(x, axis, 0, 0)  20.9 us
    pallas_call x1, Pallas kernels, token_backward(): pl.pallas_call(backward_kernel, grid=(groups,), in_specs=[pl.BlockSpec(me...  12.1 us
    pallas_call x1, Pallas kernels, token_forward(): pl.pallas_call(forward_kernel, grid=(groups,), in_specs=[pl.BlockSpec(mem...  7.84 us
    ppermute x3, starting transfers between devices, halves_of(): theirs = lax.ppermute(mine, 'col', [(i, i ^ 1) for i in range(cols)])  6.97 us
    ppermute x1, waiting for transfers between devices, local(): from_after = lax.ppermute(first, axes, down)  6.09 us
  transfers between devices with their start and end apart: 14, of which 8 were waited for; matrix products, arithmetic and copies ran while one was open for 3% of the time, Pallas kernels for 12%

profile of v2, /device:TPU:31, one launch (start us, length us, event | category | flops | bytes accessed | tf_op | source)
XLA Modules:
  0.0 193.7 jit_solution(763290043461879140)
XLA Ops:
  0.6 0.7 fusion
  1.4 3.7 %collective-permute-start = (bf16[64,128]{1,0:T(8,128)(2,1)S(1)}, bf16[64,128]{1,0:T(8,128)(2,1)S(1)}, u32[]{:S(2)}, u32[]{:S(2)}) collective-permute-start(bf16[64,128]{1,0:T(8,128)(2,1)S(1)} %get-tuple-element.85), channel_id=1, source_target_pairs={{0,1},{1,2},{2,3},{3,4},{4,5},{5,6},{6,7},{7,8},{8,9},{9,10},{10,1... | collective-permute-start | bytes 49160 | tf_op jit(solution)/shard_map/ppermute | solution.py:83
  5.0 1.9 collective-permute-start.1
  7.0 0.7 broadcast_subtract_fusion
  7.7 0.7 subtract_add_fusion.starts
  8.3 0.0 collective-permute-done.before
  8.3 6.0 %collective-permute-done.1.after = bf16[64,128]{1,0:T(8,128)(2,1)S(1)} collective-permute-done((bf16[64,128]{1,0:T(8,128)(2,1)S(1)}, bf16[64,128]{1,0:T(8,128)(2,1)S(1)}, u32[]{:S(2)}, u32[]{:S(2)}) %collective-permute-start.1) | collective-permute-done | bytes 16416 | tf_op jit(solution)/shard_map/ppermute | solution.py:84
  14.3 0.7 copy-done.7
  15.0 7.5 %atoms_forward.1 = (bf16[16,32,1024]{2,1,0:T(8,128)(2,1)}, bf16[256,128]{1,0:T(8,128)(2,1)}, f32[256,768]{1,0:T(8,128)}, bf16[256,128]{1,0:T(8,128)(2,1)}, bf16[...) custom-call(s32[8]{0:T(128)S(1)} %subtract_add_fusion.starts, ...), custom_call_target="tpu_custom_call" | custom-call | tf_op jit(solution)/shard_map/atoms_forward/pallas_call | solution.py:435
  22.4 0.0 copy-start.9
  22.5 0.0 copy-start.2
  22.5 5.3 %all-to-all-start = ((bf16[16,32,1024]{2,1,0:T(8,128)(2,1)}), bf16[16,32,1024]{2,1,0:T(8,128)(2,1)S(1)}, u32[]{:S(2)}, u32[]{:S(2)}) async-start(bf16[16,32,1024]{2,1,0:T(8,128)(2,1)} %get-tuple-element.40), calls=%async_computation | async-start | bytes 2097152 | tf_op jit(solution)/shard_map/all_to_all | solution.py:62
  27.8 0.0 copy-done.10
  27.9 0.1 dynamic-slice_bitcast_fusion
  27.9 0.1 copy.28.inverse
  28.0 0.0 copy-done.9
  28.0 12.4 %all-to-all-done.parts = bf16[16,32,1024]{2,1,0:T(8,128)(2,1)S(1)} async-done(((bf16[16,32,1024]{2,1,0:T(8,128)(2,1)}), bf16[16,32,1024]{2,1,0:T(8,128)(2,1)S(1)}, u32[]{:S(2)}, u32[]{:S(2)}) %all-to-all-start) | async-done | bytes 1048608 | tf_op jit(solution)/shard_map/all_to_all | solution.py:62
  40.5 1.1 token_norm.1
  41.6 7.3 %all-to-all-start.1 = ((bf16[8,32,768]{2,1,0:T(8,128)(2,1)}), bf16[8,32,768]{2,1,0:T(8,128)(2,1)}, u32[]{:S(2)}, u32[]{:S(2)}) async-start(bf16[8,32,768]{2,1,0:T(8,128)(2,1)} %get-tuple-element.43), calls=%async_computation.1 | async-start | bytes 786432 | tf_op jit(solution)/shard_map/all_to_all | solution.py:62
  48.8 0.0 copy-done.2
  48.8 0.0 copy-done.1
  48.8 0.0 copy-start.3
  48.9 1.3 copy-done.3
  50.1 2.9 %token_project.1 = (f32[32,768]{1,0:T(8,128)}, f32[32,768]{1,0:T(8,128)}, f32[32,768]{1,0:T(8,128)}, bf16[8,32,2304]{2,1,0:T(8,128)(2,1)}) custom-call(bf16[16,32,1024]{2,1,0:T(8,128)(2,1)S(1)} %all-to-all-done.parts, bf16[32,768]{1,0:T(8,128)(2,1)} %get-tuple-element.41.normed, bf16[768,128]{1,0:T(8,128)(2,1)} %wt2a.3, bf16[768,768]{1,0:T(8,128)(2,1)S(1)} %copy-done.3, ...), custom_call_target="tpu_custom_call" | custom-call | tf_op jit(solution)/shard_map/token_project/pallas_call | solution.py:137
  53.0 2.5 %all-to-all-done.1.keys = bf16[8,32,768]{2,1,0:T(8,128)(2,1)} async-done(((bf16[8,32,768]{2,1,0:T(8,128)(2,1)}), bf16[8,32,768]{2,1,0:T(8,128)(2,1)}, u32[]{:S(2)}, u32[]{:S(2)}) %all-to-all-start.1) | async-done | bytes 393248 | tf_op jit(solution)/shard_map/all_to_all | solution.py:62
  55.5 1.8 token_pack.1
  57.4 19.6 %all_to_all.40 = bf16[8,32,2304]{2,1,0:T(8,128)(2,1)S(1)} all-to-all(bf16[8,32,2304]{2,1,0:T(8,128)(2,1)} %token_pack.1), channel_id=1, replica_groups={{0,2,4,6,8,10,12,14},{1,3,5,7,9,11,13,15},{16,18,20,22,24,26,28,30},{17..., dimensions={0} | all-to-all | bytes 2359296 | tf_op jit(solution)/shard_map/all_to_all | solution.py:68
  77.0 2.7 %collective-permute-start.2 = (bf16[8,32,2304]{2,1,0:T(8,128)(2,1)S(1)}, bf16[8,32,2304]{2,1,0:T(8,128)(2,1)S(1)}, u32[]{:S(2)}, u32[]{:S(2)}) collective-permute-start(bf16[8,32,2304]{2,1,0:T(8,128)(2,1)S(1)} %all_to_all.40), channel_id=1, source_target_pairs={{0,1},{1,0},{2,3},{3,2},{4,5},{5,4},{6,7},{7,6},{8,9},{9,8},{10,11... | collective-permute-start | bytes 3538952 | tf_op jit(solution)/shard_map/ppermute | solution.py:74
  79.8 3.4 %token_keys.1 = (bf16[768,256]{1,0:T(8,128)(2,1)}, bf16[768,256]{1,0:T(8,128)(2,1)}) custom-call(bf16[256,2304]{1,0:T(8,128)(2,1)S(1)} %bitcast.18, bf16[768,1536]{1,0:T(8,128)(2,1)} %wv.3, bf16[768,1536]{1,0:T(8,128)(2,1)} %wv.3), custom_call_target="tpu_custom_call" | custom-call | tf_op jit(solution)/shard_map/token_keys/pallas_call | solution.py:189
  83.1 0.0 collective-permute-done.2
  83.1 0.0 copy-done
  83.1 7.8 %token_forward.1 = (bf16[512,768]{1,0:T(8,128)(2,1)}, bf16[768,512]{1,0:T(8,128)(2,1)}, bf16[512,768]{1,0:T(8,128)(2,1)}, bf16[768,512]{1,0:T(8,128)(2,1)}, bf16...) custom-call(s32[1]{0:T(128)} %bitcast.core, bf16[768,256]{1,0:T(8,128)(2,1)} %get-tuple-element.44.k_t, ...), custom_call_target="tpu_custom_call" | custom-call | tf_op jit(solution)/shard_map/token_forward/pallas_call | solution.py:266
  91.0 12.6 %all_to_all.41.mine = bf16[8,2,24,512]{3,2,1,0:T(8,128)(2,1)S(1)} all-to-all(bf16[8,2,24,512]{3,2,1,0:T(8,128)(2,1)} %get-tuple-element.46), channel_id=1, replica_groups={{0,2,4,6,8,10,12,14},{1,3,5,7,9,11,13,15},{16,18,20,22,24,26,28,30},{17..., dimensions={0} | all-to-all | bytes 786432 | tf_op jit(solution)/shard_map/all_to_all | solution.py:68
  103.6 6.4 %all-to-all-start.6 = ((bf16[16,32,768]{2,1,0:T(8,128)(2,1)}), bf16[16,32,768]{2,1,0:T(8,128)(2,1)S(1)}, u32[]{:S(2)}, u32[]{:S(2)}) async-start(bf16[16,32,768]{2,1,0:T(8,128)(2,1)} %get-tuple-element.54), calls=%async_computation.6 | async-start | bytes 1572864 | tf_op jit(solution)/shard_map/all_to_all | solution.py:62
  110.0 0.4 collective-permute-start.3
  110.3 1.4 collective-permute-done.3.theirs
  111.7 12.1 %token_backward.1 = (bf16[256,768]{1,0:T(8,128)(2,1)}, bf16[256,768]{1,0:T(8,128)(2,1)}, bf16[256,768]{1,0:T(8,128)(2,1)}) custom-call(s32[1]{0:T(128)} %bitcast.core, bf16[8,2,24,512]{3,2,1,0:T(8,128)(2,1)S(1)} %all_to_all.41.mine, bf16[8,2,24,512]{3,2,1,0:T(8,128)(2,1)S(1)} %collective-permute-done.3.theirs, bf16[512,768]{1,0:T(8,128)(2,1)} %get-tuple-element.47.q, ...), custom_call_target="tpu_custom_call" | custom-call | tf_op jit(solution)/shard_map/token_backward/pallas_call | solution.py:370
  123.8 0.4 collective-permute-start.4
  124.2 0.0 all-to-all-done.6.parts
  124.2 6.1 %all-to-all-start.5 = ((bf16[8,32,768]{2,1,0:T(8,128)(2,1)}), bf16[8,32,768]{2,1,0:T(8,128)(2,1)S(1)}, u32[]{:S(2)}, u32[]{:S(2)}) async-start(bf16[8,32,768]{2,1,0:T(8,128)(2,1)} %bitcast.30), calls=%async_computation.5 | async-start | bytes 786432 | tf_op jit(solution)/shard_map/all_to_all | solution.py:62
  130.3 0.0 collective-permute-done.4
  130.3 1.8 add_convert_fusion
  132.2 5.9 %all-to-all-done.5.parts = bf16[8,32,768]{2,1,0:T(8,128)(2,1)S(1)} async-done(((bf16[8,32,768]{2,1,0:T(8,128)(2,1)}), bf16[8,32,768]{2,1,0:T(8,128)(2,1)S(1)}, u32[]{:S(2)}, u32[]{:S(2)}) %all-to-all-start.5) | async-done | bytes 393248 | tf_op jit(solution)/shard_map/all_to_all | solution.py:62
  138.1 5.1 %all-to-all-start.4 = ((bf16[8,32,768]{2,1,0:T(8,128)(2,1)}), bf16[8,32,768]{2,1,0:T(8,128)(2,1)S(1)}, u32[]{:S(2)}, u32[]{:S(2)}) async-start(bf16[8,32,768]{2,1,0:T(8,128)(2,1)} %bitcast.10), calls=%async_computation.4 | async-start | bytes 786432 | tf_op jit(solution)/shard_map/all_to_all | solution.py:68
  143.2 0.1 token_keyval.1
  143.3 3.3 %collective-permute-start.5 = (bf16[32,768]{1,0:T(8,128)(2,1)S(1)}, bf16[32,768]{1,0:T(8,128)(2,1)S(1)}, u32[]{:S(2)}, u32[]{:S(2)}) collective-permute-start(bf16[32,768]{1,0:T(8,128)(2,1)S(1)} %token_keyval.1), channel_id=1, source_target_pairs={{0,0},{1,1},{16,2},{17,3},{32,4},{33,5},{48,6},{49,7},{64,8},{65,9... | collective-permute-start | bytes 147464 | tf_op jit(solution)/shard_map/ppermute | solution.py:831
  146.6 0.1 pad_add_fusion.1.place
  146.6 4.3 %token_own.1 = (bf16[32,768]{1,0:T(8,128)(2,1)S(1)}, bf16[32,128]{1,0:T(8,128)(2,1)S(1)}, f32[32,768]{1,0:T(8,128)S(1)}) custom-call(s32[2]{0:T(128)S(1)} %pad_add_fusion.1.place, bf16[16,32,768]{2,1,0:T(8,128)(2,1)S(1)} %all-to-all-done.6.parts, bf16[8,2,24,512]{3,2,1,0:T(8,128)(2,1)S(1)} %all_to_all.41.mine, ...), custom_call_target="tpu_custom_call" | custom-call | tf_op jit(solution)/shard_map/token_own/pallas_call | solution.py:435
  151.0 0.4 collective-permute-done.5.key_feature
  151.4 0.0 all-to-all-done.4.parts
  151.4 2.9 %token_grads.1 = bf16[8,32,992]{2,1,0:T(8,128)(2,1)} custom-call(bf16[8,32,768]{2,1,0:T(8,128)(2,1)S(1)} %all-to-all-done.4.parts, bf16[32,768]{1,0:T(8,128)(2,1)S(1)} %collective-permute-done.5.key_feature, f32[32,768]{1,0:T(8,128)S(1)} %get-tuple-element.58.feature, f32[32,768]{1,0:T(8,128)} %get-tuple-element.59.grad_new, ...), custom_call_target="tpu_custom_call" | custom-call | tf_op jit(solution)/shard_map/token_grads/pallas_call | solution.py:435
  154.3 11.3 %all_to_all.42 = bf16[8,32,992]{2,1,0:T(8,128)(2,1)S(1)} all-to-all(bf16[8,32,992]{2,1,0:T(8,128)(2,1)} %token_grads.1), channel_id=1, replica_groups={{0,2,4,6,8,10,12,14},{1,3,5,7,9,11,13,15},{16,18,20,22,24,26,28,30},{17..., dimensions={0} | all-to-all | bytes 1015808 | tf_op jit(solution)/shard_map/all_to_all | solution.py:68
  165.6 3.9 %collective-permute-start.6 = (bf16[8,32,992]{2,1,0:T(8,128)(2,1)S(1)}, bf16[8,32,992]{2,1,0:T(8,128)(2,1)S(1)}, u32[]{:S(2)}, u32[]{:S(2)}) collective-permute-start(bf16[8,32,992]{2,1,0:T(8,128)(2,1)S(1)} %all_to_all.42), channel_id=1, source_target_pairs={{0,1},{1,0},{2,3},{3,2},{4,5},{5,4},{6,7},{7,6},{8,9},{9,8},{10,11... | collective-permute-start | bytes 1523720 | tf_op jit(solution)/shard_map/ppermute | solution.py:74
  169.4 0.1 copy.29.token
  169.6 0.1 pad_add_fusion.place
  169.7 1.3 collective-permute-done.6
  171.0 5.6 %atoms_backward.1 = (bf16[256,128]{1,0:T(8,128)(2,1)}, bf16[512,48]{1,0:T(8,128)(2,1)S(1)}, bf16[512,48]{1,0:T(8,128)(2,1)S(1)}, f32[256,256]{1,0:T(8,128)}, bf1...) custom-call(s32[8]{0:T(128)S(1)} %subtract_add_fusion.starts, ...), custom_call_target="tpu_custom_call" | custom-call | tf_op jit(solution)/shard_map/atoms_backward/pallas_call | solution.py:435
  176.6 5.5 %collective-permute-start.7 = (bf16[64,256]{1,0:T(8,128)(2,1)S(1)}, bf16[64,256]{1,0:T(8,128)(2,1)S(1)}, u32[]{:S(2)}, u32[]{:S(2)}) collective-permute-start(bf16[64,256]{1,0:T(8,128)(2,1)S(1)} %get-tuple-element.71), channel_id=1, source_target_pairs={{0,1},{1,2},{2,3},{3,4},{4,5},{5,6},{6,7},{7,8},{8,9},{9,10},{10,1... | collective-permute-start | bytes 98312 | tf_op jit(solution)/shard_map/ppermute | solution.py:887
  182.2 1.9 collective-permute-start.8
  184.1 0.7 copy.30
  184.8 0.7 copy.31
  185.5 0.0 collective-permute-done.7.before
  185.5 6.1 %collective-permute-done.8.after = bf16[64,256]{1,0:T(8,128)(2,1)S(1)} collective-permute-done((bf16[64,256]{1,0:T(8,128)(2,1)S(1)}, bf16[64,256]{1,0:T(8,128)(2,1)S(1)}, u32[]{:S(2)}, u32[]{:S(2)}) %collective-permute-start.8) | collective-permute-done | bytes 32800 | tf_op jit(solution)/shard_map/ppermute | solution.py:888
  191.6 2.0 %atoms_last.1 = bf16[256,128]{1,0:T(8,128)(2,1)} custom-call(f32[256,256]{1,0:T(8,128)} %get-tuple-element.70.inner, bf16[64,256]{1,0:T(8,128)(2,1)S(1)} %collective-permute-done.7.before, bf16[64,256]{1,0:T(8,128)(2,1)S(1)} %collective-permute-done.8.after, f32[256,128]{1,0:T(8,128)} %get-tuple-element.73.feature, f32[256,128]{1,0:T(8,128)} %get-tuple-element.74.atoms_grad, ...), custom_call_target="tpu_custom_call" | custom-call | tf_op jit(solution)/shard_map/atoms_last/pallas_call | solution.py:435
  (14 shorter events, 0.0 us)
Async XLA Ops:
  1.4 7.0 %collective-permute-start = (bf16[64,128]{1,0:T(8,128)(2,1)S(1)}, bf16[64,128]{1,0:T(8,128)(2,1)S(1)}, u32[]{:S(2)}, u32[]{:S(2)}) collective-permute-start(bf16[64,128]{1,0:T(8,128)(2,1)S(1)} %get-tuple-element.85), channel_id=1, source_target_pairs={{0,1},{1,2},{2,3},{3,4},{4,5},{5,6},{6,7},{7,8},{8,9},{9,10},{10,1... | collective-permute-start | bytes 49160 | tf_op jit(solution)/shard_map/ppermute | solution.py:83
  5.0 9.3 %collective-permute-start.1 = (bf16[64,128]{1,0:T(8,128)(2,1)S(1)}, bf16[64,128]{1,0:T(8,128)(2,1)S(1)}, u32[]{:S(2)}, u32[]{:S(2)}) collective-permute-start(bf16[64,128]{1,0:T(8,128)(2,1)S(1)} %get-tuple-element.84), channel_id=1, source_target_pairs={{1,0},{2,1},{3,2},{4,3},{5,4},{6,5},{7,6},{8,7},{9,8},{10,9},{11,1... | collective-permute-start | bytes 49160 | tf_op jit(solution)/shard_map/ppermute | solution.py:84
  14.3 0.7 copy-start.7
  22.4 5.4 %copy-start.10 = (s32[512]{0:T(512)S(1)}, s32[512]{0:T(512)}, u32[]{:S(2)}) copy-start(s32[512]{0:T(512)} %param.25) | copy-start | bytes 6148
  22.4 5.6 %copy-start.9 = (f32[768]{0:T(1024)S(1)}, f32[768]{0:T(1024)}, u32[]{:S(2)}) copy-start(f32[768]{0:T(1024)} %param.32) | copy-start | bytes 9220
  22.5 26.4 %copy-start.2 = (bf16[768,768]{1,0:T(8,128)(2,1)S(1)}, bf16[768,768]{1,0:T(8,128)(2,1)}, u32[]{:S(2)}) copy-start(bf16[768,768]{1,0:T(8,128)(2,1)} %wout.3) | copy-start | bytes 3538948
  22.5 18.0 %all-to-all-start = ((bf16[16,32,1024]{2,1,0:T(8,128)(2,1)}), bf16[16,32,1024]{2,1,0:T(8,128)(2,1)S(1)}, u32[]{:S(2)}, u32[]{:S(2)}) async-start(bf16[16,32,1024]{2,1,0:T(8,128)(2,1)} %get-tuple-element.40), calls=%async_computation | async-start | bytes 2097152 | tf_op jit(solution)/shard_map/all_to_all | solution.py:62
  27.8 21.0 %copy-start.1 = (bf16[768,768]{1,0:T(8,128)(2,1)S(1)}, bf16[768,768]{1,0:T(8,128)(2,1)}, u32[]{:S(2)}) copy-start(bf16[768,768]{1,0:T(8,128)(2,1)} %wgate.1) | copy-start | bytes 3538948
  41.6 14.0 %all-to-all-start.1 = ((bf16[8,32,768]{2,1,0:T(8,128)(2,1)}), bf16[8,32,768]{2,1,0:T(8,128)(2,1)}, u32[]{:S(2)}, u32[]{:S(2)}) async-start(bf16[8,32,768]{2,1,0:T(8,128)(2,1)} %get-tuple-element.43), calls=%async_computation.1 | async-start | bytes 786432 | tf_op jit(solution)/shard_map/all_to_all | solution.py:62
  48.8 1.3 copy-start.3
  77.0 6.1 %collective-permute-start.2 = (bf16[8,32,2304]{2,1,0:T(8,128)(2,1)S(1)}, bf16[8,32,2304]{2,1,0:T(8,128)(2,1)S(1)}, u32[]{:S(2)}, u32[]{:S(2)}) collective-permute-start(bf16[8,32,2304]{2,1,0:T(8,128)(2,1)S(1)} %all_to_all.40), channel_id=1, source_target_pairs={{0,1},{1,0},{2,3},{3,2},{4,5},{5,4},{6,7},{7,6},{8,9},{9,8},{10,11... | collective-permute-start | bytes 3538952 | tf_op jit(solution)/shard_map/ppermute | solution.py:74
  79.8 3.4 %copy-start = (bf16[16,512,256]{2,1,0:T(8,128)(2,1)S(1)}, bf16[16,512,256]{2,1,0:T(8,128)(2,1)}, u32[]{:S(2)}) copy-start(bf16[16,512,256]{2,1,0:T(8,128)(2,1)} %bias.3) | copy-start | bytes 12582916
  103.6 20.7 %all-to-all-start.6 = ((bf16[16,32,768]{2,1,0:T(8,128)(2,1)}), bf16[16,32,768]{2,1,0:T(8,128)(2,1)S(1)}, u32[]{:S(2)}, u32[]{:S(2)}) async-start(bf16[16,32,768]{2,1,0:T(8,128)(2,1)} %get-tuple-element.54), calls=%async_computation.6 | async-start | bytes 1572864 | tf_op jit(solution)/shard_map/all_to_all | solution.py:62
  110.0 1.7 collective-permute-start.3
  123.8 6.6 %collective-permute-start.4 = (bf16[256,768]{1,0:T(8,128)(2,1)}, bf16[256,768]{1,0:T(8,128)(2,1)S(1)}, u32[]{:S(2)}, u32[]{:S(2)}) collective-permute-start(bf16[256,768]{1,0:T(8,128)(2,1)} %get-tuple-element.52), channel_id=1, source_target_pairs={{0,1},{1,0},{2,3},{3,2},{4,5},{5,4},{6,7},{7,6},{8,9},{9,8},{10,11... | collective-permute-start | bytes 1179656 | tf_op jit(solution)/shard_map/ppermute | solution.py:803
  124.2 13.9 %all-to-all-start.5 = ((bf16[8,32,768]{2,1,0:T(8,128)(2,1)}), bf16[8,32,768]{2,1,0:T(8,128)(2,1)S(1)}, u32[]{:S(2)}, u32[]{:S(2)}) async-start(bf16[8,32,768]{2,1,0:T(8,128)(2,1)} %bitcast.30), calls=%async_computation.5 | async-start | bytes 786432 | tf_op jit(solution)/shard_map/all_to_all | solution.py:62
  138.1 13.3 %all-to-all-start.4 = ((bf16[8,32,768]{2,1,0:T(8,128)(2,1)}), bf16[8,32,768]{2,1,0:T(8,128)(2,1)S(1)}, u32[]{:S(2)}, u32[]{:S(2)}) async-start(bf16[8,32,768]{2,1,0:T(8,128)(2,1)} %bitcast.10), calls=%async_computation.4 | async-start | bytes 786432 | tf_op jit(solution)/shard_map/all_to_all | solution.py:68
  143.3 8.2 %collective-permute-start.5 = (bf16[32,768]{1,0:T(8,128)(2,1)S(1)}, bf16[32,768]{1,0:T(8,128)(2,1)S(1)}, u32[]{:S(2)}, u32[]{:S(2)}) collective-permute-start(bf16[32,768]{1,0:T(8,128)(2,1)S(1)} %token_keyval.1), channel_id=1, source_target_pairs={{0,0},{1,1},{16,2},{17,3},{32,4},{33,5},{48,6},{49,7},{64,8},{65,9... | collective-permute-start | bytes 147464 | tf_op jit(solution)/shard_map/ppermute | solution.py:831
  151.4 19.6 %copy-start.5 = (bf16[8,128,256]{2,1,0:T(8,128)(2,1)S(1)}, bf16[8,128,256]{2,1,0:T(8,128)(2,1)}, u32[]{:S(2)}) copy-start(bf16[8,128,256]{2,1,0:T(8,128)(2,1)} %get-tuple-element.65.window) | copy-start | bytes 1572868
  151.4 19.6 %copy-start.6 = (f32[8,128,128]{2,1,0:T(8,128)S(1)}, f32[8,128,128]{2,1,0:T(8,128)}, u32[]{:S(2)}) copy-start(f32[8,128,128]{2,1,0:T(8,128)} %get-tuple-element.66.prob) | copy-start | bytes 1572868
  154.3 16.7 %copy-start.4 = (f32[256,768]{1,0:T(8,128)S(1)}, f32[256,768]{1,0:T(8,128)}, u32[]{:S(2)}) copy-start(f32[256,768]{1,0:T(8,128)} %get-tuple-element.62.slope) | copy-start | bytes 2359300
  165.6 5.4 %collective-permute-start.6 = (bf16[8,32,992]{2,1,0:T(8,128)(2,1)S(1)}, bf16[8,32,992]{2,1,0:T(8,128)(2,1)S(1)}, u32[]{:S(2)}, u32[]{:S(2)}) collective-permute-start(bf16[8,32,992]{2,1,0:T(8,128)(2,1)S(1)} %all_to_all.42), channel_id=1, source_target_pairs={{0,1},{1,0},{2,3},{3,2},{4,5},{5,4},{6,7},{7,6},{8,9},{9,8},{10,11... | collective-permute-start | bytes 1523720 | tf_op jit(solution)/shard_map/ppermute | solution.py:74
  171.0 20.6 %copy-start.8 = (f32[128]{0:T(128)S(1)}, f32[128]{0:T(128)}, u32[]{:S(2)}) copy-start(f32[128]{0:T(128)} %param.27) | copy-start | bytes 1540
  176.6 8.9 %collective-permute-start.7 = (bf16[64,256]{1,0:T(8,128)(2,1)S(1)}, bf16[64,256]{1,0:T(8,128)(2,1)S(1)}, u32[]{:S(2)}, u32[]{:S(2)}) collective-permute-start(bf16[64,256]{1,0:T(8,128)(2,1)S(1)} %get-tuple-element.71), channel_id=1, source_target_pairs={{0,1},{1,2},{2,3},{3,4},{4,5},{5,6},{6,7},{7,8},{8,9},{9,10},{10,1... | collective-permute-start | bytes 98312 | tf_op jit(solution)/shard_map/ppermute | solution.py:887
  182.2 9.5 %collective-permute-start.8 = (bf16[64,256]{1,0:T(8,128)(2,1)S(1)}, bf16[64,256]{1,0:T(8,128)(2,1)S(1)}, u32[]{:S(2)}, u32[]{:S(2)}) collective-permute-start(bf16[64,256]{1,0:T(8,128)(2,1)S(1)} %get-tuple-element.72), channel_id=1, source_target_pairs={{1,0},{2,1},{3,2},{4,3},{5,4},{6,5},{7,6},{8,7},{9,8},{10,9},{11,1... | collective-permute-start | bytes 98312 | tf_op jit(solution)/shard_map/ppermute | solution.py:888
